TPU v7x, 512 devices: a whole 4x4x16 slice. The times are simulated.
512 devices in a mesh: slab: 8 (over y_hi, x), walker: 16 (over z), geom: 4 (over y_lo, core).
Axes of the slice: x: 4, y: 4 (y_hi: 2, y_lo: 2; y = y_hi * 2 + y_lo), z: 16, core: 2. Of those that a mesh axis runs over, the one named last changes fastest.
Arguments:
- features: bfloat16 [4, 32, 1024, 256], P('geom', 'walker', 'slab'), may hold values from -6 to 6
- w_self: bfloat16 [256, 256], replicated, may hold values from -0.375 to 0.375
- w_pair: bfloat16 [256, 256], replicated, may hold values from -0.375 to 0.375
- w_update: bfloat16 [256, 256], replicated, may hold values from -0.375 to 0.375
- geo_embed: float32 [4, 2, 256], P('geom'), may hold values from -6 to 6
- lattice: int32 [4, 32], P('geom', 'walker'), may hold values from 0 to 1
- neighbours: int32 [4, 32, 1024, 64], P('geom', 'walker', 'slab'), may hold values from 0 to 191, as said below
- counts: int32 [4, 32, 1024], P('geom', 'walker', 'slab'), may hold values from 1 to 64
- envelope: bfloat16 [4, 32, 1024, 64], P('geom', 'walker', 'slab'), may hold values from 0.099609375 to 1
- cotangent: bfloat16 [4, 32, 1024, 256], P('geom', 'walker', 'slab'), may hold values from -6 to 6
Outputs:
- new_features: bfloat16 [4, 32, 1024, 256], P('geom', 'walker', 'slab')
- d_features: float32 [4, 32, 1024, 256], P('geom', 'walker', 'slab')
- d_w_self: float32 [256, 256], P('walker')
- d_w_pair: float32 [256, 256], P('walker')
- d_w_update: float32 [256, 256], P('walker')
- d_geo: float32 [4, 2, 256], P('geom')
Inputs may be any that keep to these rules, and one draw needn't show every extreme that they name: `neighbours`: for an electron at position l within its slab, every entry lies within l to l + 64 and differs from l + 32.
All inputs are finite; a program needn't handle non-finite values.
Results may differ from a plain program's by a relative error of at most 0.0055.
Values may be sent and summed in bfloat16 or wider, within the bound.
A program may use at most 64 MiB of HBM per device.

v0:
```python
import jax
import jax.numpy as jnp
from jax import lax
from jax.sharding import PartitionSpec as P

RIM = 32


def extended(value, sides, width):
    for axis, dim in sides:
        size, length = (lax.axis_size(axis), value.shape[dim])
        up = [(i, (i + 1) % size) for i in range(size)]
        down = [(j, i) for i, j in up]
        last = lax.slice_in_dim(value, length - width, length, axis=dim)
        first = lax.slice_in_dim(value, 0, width, axis=dim)
        before = lax.ppermute(last, axis, up)
        after = lax.ppermute(first, axis, down)
        value = jnp.concatenate([before, value, after], axis=dim)
    return value


def shifted(block, axis, distance):
    devices = range(lax.axis_size(axis))
    route = [((i - distance) % len(devices), i) for i in devices]
    return lax.ppermute(block, axis, route)


def silu_grad(value):
    sig = jax.nn.sigmoid(value)
    return sig * (1.0 + value * (1.0 - sig))


def body(
    features, w_self, w_pair, w_update, geo_embed, lattice, neighbours, counts, envelope, cotangent
):
    feats = features[0]
    rows = feats.shape[1]
    width = feats.shape[2]
    slots = neighbours.shape[3]
    lats = geo_embed.shape[1]
    blocks = rows // RIM
    span = 3 * RIM
    select = (lattice[0][:, None] == jnp.arange(lats)[None, :]).astype(jnp.float32)
    geo_rows = jnp.dot(select, geo_embed[0], precision=lax.Precision.HIGHEST)
    p_all = (
        jnp.einsum("wed,df->wef", feats, w_self, preferred_element_type=jnp.float32)
        + geo_rows[:, None, :]
    )
    q_local = jnp.einsum("wed,df->wef", feats, w_pair, preferred_element_type=jnp.float32).astype(
        jnp.bfloat16
    )
    q_ext = extended(q_local, (("slab", 1),), RIM)
    block_base = jnp.arange(blocks) * RIM
    window_pos = jnp.arange(span)

    def walker_work(inputs):
        own, q_rows, p_rows, nbr, cnt, env, dout = inputs
        q_blocks = q_rows.reshape(blocks + 2, RIM, width)
        windows = jnp.concatenate(
            (q_blocks[:blocks], q_blocks[1 : blocks + 1], q_blocks[2 : blocks + 2]), axis=1
        )
        local_nbr = nbr.reshape(blocks, RIM, slots) - block_base[:, None, None]
        onehot = local_nbr[..., None] == window_pos[None, None, None, :]
        gathered = jnp.einsum(
            "bksm,bmf->bksf",
            onehot.astype(jnp.bfloat16),
            windows,
            preferred_element_type=jnp.float32,
        )
        pre = p_rows[:, None, :] + gathered.reshape(rows, slots, width)
        valid = (jnp.arange(slots)[None, :] < cnt[:, None]).astype(jnp.float32)
        weight = env.astype(jnp.float32) * valid
        denom = cnt[:, None].astype(jnp.float32)
        agg = (jnp.sum(jax.nn.silu(pre) * weight[:, :, None], axis=1) / denom).astype(jnp.bfloat16)
        upd = jnp.dot(agg, w_update, preferred_element_type=jnp.float32)
        new_rows = (own.astype(jnp.float32) + jax.nn.silu(upd)).astype(jnp.bfloat16)
        d_upd = (dout.astype(jnp.float32) * silu_grad(upd)).astype(jnp.bfloat16)
        d_agg = jnp.dot(d_upd, w_update.T, preferred_element_type=jnp.float32)
        d_pre = (d_agg / denom)[:, None, :] * weight[:, :, None] * silu_grad(pre)
        d_self = jnp.sum(d_pre, axis=1)
        d_window = jnp.einsum(
            "bksm,bksf->bmf",
            onehot.astype(jnp.float32),
            d_pre.reshape(blocks, RIM, slots, width),
            precision=lax.Precision.HIGHEST,
        )
        d_window = d_window.reshape(blocks, 3, RIM, width)
        d_blocks = jnp.pad(d_window[:, 0], ((0, 2), (0, 0), (0, 0)))
        d_blocks = d_blocks + jnp.pad(d_window[:, 1], ((1, 1), (0, 0), (0, 0)))
        d_blocks = d_blocks + jnp.pad(d_window[:, 2], ((2, 0), (0, 0), (0, 0)))
        d_pair = d_blocks.reshape(rows + 2 * RIM, width)
        return (new_rows, agg, d_upd, d_self, d_pair)

    new_rows, agg, d_upd, d_self, d_pair_ext = lax.map(
        walker_work, (feats, q_ext, p_all, neighbours[0], counts[0], envelope[0], cotangent[0])
    )
    lower = d_pair_ext[:, :RIM]
    upper = d_pair_ext[:, RIM + rows :]
    middle = d_pair_ext[:, RIM : RIM + rows]
    from_next = shifted(lower.astype(jnp.bfloat16), "slab", -1).astype(lower.dtype)
    from_prev = shifted(upper.astype(jnp.bfloat16), "slab", 1).astype(upper.dtype)
    middle = middle.at[:, rows - RIM :].add(from_next)
    middle = middle.at[:, :RIM].add(from_prev)
    dp_b = d_self.astype(jnp.bfloat16)
    dq_b = middle.astype(jnp.bfloat16)
    d_feats = (
        cotangent[0].astype(jnp.float32)
        + jnp.einsum("wef,df->wed", dp_b, w_self, preferred_element_type=jnp.float32)
        + jnp.einsum("wef,df->wed", dq_b, w_pair, preferred_element_type=jnp.float32)
    )
    grad_self = jnp.einsum("wed,wef->df", feats, dp_b, preferred_element_type=jnp.float32)
    grad_pair = jnp.einsum("wed,wef->df", feats, dq_b, preferred_element_type=jnp.float32)
    grad_update = jnp.einsum("wed,wef->df", agg, d_upd, preferred_element_type=jnp.float32)
    geo_local = jnp.dot(select.T, jnp.sum(d_self, axis=1), precision=lax.Precision.HIGHEST)
    geo_total = lax.psum(geo_local, ("slab", "walker"))
    partial_rows = (
        lax.psum_scatter(grad_self, "walker", scatter_dimension=0, tiled=True),
        lax.psum_scatter(grad_pair, "walker", scatter_dimension=0, tiled=True),
        lax.psum_scatter(grad_update, "walker", scatter_dimension=0, tiled=True),
    )
    shares = lax.psum((partial_rows[0], partial_rows[1], partial_rows[2]), ("slab", "geom"))
    return (new_rows[None], d_feats[None], shares[0], shares[1], shares[2], geo_total[None])


def solution(mesh):
    return jax.shard_map(
        body,
        mesh=mesh,
        in_specs=(
            P("geom", "walker", "slab", None),
            P(),
            P(),
            P(),
            P("geom", None, None),
            P("geom", "walker"),
            P("geom", "walker", "slab", None),
            P("geom", "walker", "slab"),
            P("geom", "walker", "slab", None),
            P("geom", "walker", "slab", None),
        ),
        out_specs=(
            P("geom", "walker", "slab", None),
            P("geom", "walker", "slab", None),
            P("walker", None),
            P("walker", None),
            P("walker", None),
            P("geom", None, None),
        ),
        check_vma=False,
    )
```

profile of v0, /device:TPU:1, one launch (start us, length us, event | category | flops | bytes accessed | tf_op | source)
XLA Modules:
  0.0 569.2 jit_solution(236864451426643334)
XLA Ops:
  7.2 0.0 copy-start
  7.2 0.0 reduce-scatter.10.cloned.1.call-start
  7.2 1.2 convolution_convert_fusion
  8.4 3.9 collective-permute-start
  12.4 5.8 %collective-permute-start.1 = (bf16[2,32,256]{2,1,0:T(8,128)(2,1)S(1)}, bf16[2,32,256]{2,1,0:T(8,128)(2,1)S(1)}, u32[]{:S(2)}, u32[]{:S(2)}) collective-permute-start(bf16[2,32,256]{2,1,0:T(8,128)(2,1)S(1)} %get-tuple-element.328), channel_id=1, source_target_pairs={{64,0},{128,64},{192,128},{256,192},{320,256},{384,320},{448,384},... | collective-permute-start | bytes 98312 | tf_op jit(solution)/shard_map/ppermute | solution.py:17
  18.2 0.9 fusion.29
  19.1 1.1 convolution_add_fusion.2
  20.3 0.9 copy.28
  21.1 0.9 copy.27
  22.1 0.0 copy-start.5
  22.1 0.0 copy-start.2
  22.1 31.5 %while.23 = (s32[]{:T(128)}, bf16[2,128,256]{2,1,0:T(8,128)(2,1)S(1)}, bf16[2,128,256]{2,1,0:T(8,128)(2,1)S(1)}, bf16[2,128,256]{2,1,0:T(8,128)(2,1)S(1)}, f32[2...) while((s32[]{:T(128)}, ...), condition=%wide.region_3.4_spmd.clone, body=%wide.region_0.3_spmd.clone.sunk | while | flops 2892726272 | bytes 40653668 | solution.py:94
  22.2 0.7 convert_bitcast_fusion.2
  22.9 0.1 lt.47
  23.0 0.1 convert_select_fusion.2
  23.1 0.1 broadcast_subtract_fusion.2
  23.2 0.0 copy-start.1
  23.2 0.0 copy-start.3
  23.3 0.0 copy-start.4
  23.3 3.7 multiply_reduce_fusion.2
  27.0 0.1 fusion.63
  27.1 0.1 fusion.64
  27.2 0.2 bitcast_dynamic-update-slice_fusion.7
  27.5 0.2 convolution_divide_fusion.2
  27.7 4.1 fusion.65
  31.8 6.0 %fusion.66 = f32[4,96,256,1]{2,1,3,0:T(8,128)S(1)} fusion(f32[4,32,64,256]{3,2,1,0:T(8,128)S(1)} %get-tuple-element.440, s32[4,32,64]{2,1,0:T(8,128)S(1)} %broadcast_subtract_fusion.2), kind=kOutput, calls=%fused_computation.6.clone.1 | convolution fusion | flops 2416705536 | bytes 8814592 | tf_op jit(solution)/shard_map/while/body/eval_jaxpr/bksm,bksf->bmf/dot_general | solution.py:81
  37.9 0.7 convert_bitcast_fusion.2
  38.6 0.1 lt.47
  38.7 0.1 convert_select_fusion.2
  38.8 0.1 broadcast_subtract_fusion.2
  39.0 0.0 copy-start.1
  39.0 0.0 copy-start.3
  39.0 0.0 copy-start.4
  39.0 3.7 multiply_reduce_fusion.2
  42.7 0.1 fusion.63
  42.8 0.1 fusion.64
  43.0 0.2 bitcast_dynamic-update-slice_fusion.7
  43.2 0.2 convolution_divide_fusion.2
  43.4 4.1 fusion.65
  47.6 6.0 %fusion.66 = f32[4,96,256,1]{2,1,3,0:T(8,128)S(1)} fusion(f32[4,32,64,256]{3,2,1,0:T(8,128)S(1)} %get-tuple-element.440, s32[4,32,64]{2,1,0:T(8,128)S(1)} %broadcast_subtract_fusion.2), kind=kOutput, calls=%fused_computation.6.clone.1 | convolution fusion | flops 2416705536 | bytes 8814592 | tf_op jit(solution)/shard_map/while/body/eval_jaxpr/bksm,bksf->bmf/dot_general | solution.py:81
  53.6 0.0 copy-start.6
  53.7 1.9 collective-permute-start.3
  55.7 7.0 %collective-permute-start.2 = (bf16[2,32,256]{2,1,0:T(8,128)(2,1)S(1)}, bf16[2,32,256]{2,1,0:T(8,128)(2,1)S(1)}, u32[]{:S(2)}, u32[]{:S(2)}) collective-permute-start(bf16[2,32,256]{2,1,0:T(8,128)(2,1)S(1)} %get-tuple-element.326), channel_id=1, source_target_pairs={{64,0},{128,64},{192,128},{256,192},{320,256},{384,320},{448,384},... | collective-permute-start | bytes 98312 | tf_op jit(solution)/shard_map/ppermute | solution.py:25
  62.6 1.1 convolution_bitcast_fusion.2
  63.8 0.8 copy.39
  64.6 0.0 reduce-scatter.10.cloned.1.call-update
  64.6 0.0 reduce-scatter.12.cloned.1.call-start
  64.7 1.1 convolution_bitcast_fusion.1
  65.9 0.8 copy.41
  66.7 0.0 reduce-scatter.12.cloned.1.call-update
  66.7 0.0 reduce-scatter.8.cloned.1.call-start
  66.8 0.9 convolution_bitcast_fusion
  67.7 0.0 reduce-scatter.8.cloned.1.call-update
  67.8 0.3 convolution_bitcast_fusion.3
  68.0 310.3 %psum.31 = f32[1,2,256]{2,1,0:T(2,128)} all-reduce(f32[1,2,256]{2,1,0:T(2,128)S(1)} %convolution_bitcast_fusion.3), channel_id=1, replica_groups=mesh['slab'=8,'walker'=16,'geom'=4] {'slab','walker'}, use_global_device_ids=true, to_apply=%region_11.12 | all-reduce | flops 512 | bytes 4096 | tf_op jit(solution)/shard_map/psum | solution.py:115
  378.4 1.1 convolution_add_fusion.1
  379.5 0.9 fusion.19
  380.4 0.8 copy.40
  381.2 0.0 reduce-scatter.12.cloned.1.call-done
  381.3 0.8 copy.42
  382.1 0.0 reduce-scatter.8.cloned.1.call-done
  382.1 179.2 %all-reduce.3 = (f32[16,256]{0,1:T(8,128)S(1)}, f32[16,256]{0,1:T(8,128)S(1)}, f32[16,256]{1,0:T(8,128)}) all-reduce(f32[16,256]{0,1:T(8,128)S(1)} %copy.40, f32[16,256]{0,1:T(8,128)S(1)} %copy.42, f32[16,256]{1,0:T(8,128)} %reduce-scatter.8.cloned.1.call-done), channel_id=1, replica_groups=mesh['slab'=8,'walker'=16,'geom'=4] {'slab','geom'}, use_global_device_ids=true, to_apply=%region_5.6 | all-reduce | flops 12288 | bytes 98304 | tf_op jit(solution)/shard_map/psum | solution.py:121
  561.3 0.7 copy.32
  561.9 0.7 copy.33
  (46 shorter events, 0.5 us)
Async XLA Ops:
  7.2 11.9 %copy-start = (bf16[256,256]{1,0:T(8,128)(2,1)S(1)}, bf16[256,256]{1,0:T(8,128)(2,1)}, u32[]{:S(2)}) copy-start(bf16[256,256]{1,0:T(8,128)(2,1)} %param.17) | copy-start | bytes 393220
  7.2 373.2 %reduce-scatter.10.cloned.1.call-start = ((), (), s32[]{:S(2)}) async-start(), calls=%async_computation.4 | async-start | bytes 278528
  8.4 13.7 %collective-permute-start = (bf16[2,32,256]{2,1,0:T(8,128)(2,1)S(1)}, bf16[2,32,256]{2,1,0:T(8,128)(2,1)S(1)}, u32[]{:S(2)}, u32[]{:S(2)}) collective-permute-start(bf16[2,32,256]{2,1,0:T(8,128)(2,1)S(1)} %get-tuple-element.327), channel_id=1, source_target_pairs={{0,64},{64,128},{128,192},{192,256},{256,320},{320,384},{384,448},... | collective-permute-start | bytes 98312 | tf_op jit(solution)/shard_map/ppermute | solution.py:16
  12.4 9.7 %collective-permute-start.1 = (bf16[2,32,256]{2,1,0:T(8,128)(2,1)S(1)}, bf16[2,32,256]{2,1,0:T(8,128)(2,1)S(1)}, u32[]{:S(2)}, u32[]{:S(2)}) collective-permute-start(bf16[2,32,256]{2,1,0:T(8,128)(2,1)S(1)} %get-tuple-element.328), channel_id=1, source_target_pairs={{64,0},{128,64},{192,128},{256,192},{320,256},{384,320},{448,384},... | collective-permute-start | bytes 98312 | tf_op jit(solution)/shard_map/ppermute | solution.py:17
  22.1 45.6 %copy-start.5 = (s32[1,2]{1,0:T(1,128)S(1)}, s32[1,2]{1,0:T(1,128)}, u32[]{:S(2)}) copy-start(s32[1,2]{1,0:T(1,128)} %param.21) | copy-start | bytes 28
  22.1 357.3 %copy-start.2 = (bf16[256,256]{1,0:T(8,128)(2,1)S(1)}, bf16[256,256]{1,0:T(8,128)(2,1)}, u32[]{:S(2)}) copy-start(bf16[256,256]{1,0:T(8,128)(2,1)} %param.18) | copy-start | bytes 393220
  23.2 4.0 copy-start.1
  23.2 4.0 copy-start.3
  23.3 4.0 copy-start.4
  39.0 4.0 copy-start.1
  39.0 4.0 copy-start.3
  39.0 4.0 copy-start.4
  53.6 509.0 %copy-start.6 = (bf16[2,128,256]{2,1,0:T(8,128)(2,1)}, bf16[2,128,256]{2,1,0:T(8,128)(2,1)S(1)}, u32[]{:S(2)}) copy-start(bf16[2,128,256]{2,1,0:T(8,128)(2,1)S(1)} %get-tuple-element.231) | copy-start | bytes 393220
  53.7 11.0 %collective-permute-start.3 = (bf16[2,32,256]{2,1,0:T(8,128)(2,1)S(1)}, bf16[2,32,256]{2,1,0:T(8,128)(2,1)S(1)}, u32[]{:S(2)}, u32[]{:S(2)}) collective-permute-start(bf16[2,32,256]{2,1,0:T(8,128)(2,1)S(1)} %get-tuple-element.325), channel_id=1, source_target_pairs={{448,0},{0,64},{64,128},{128,192},{192,256},{256,320},{320,384},{3... | collective-permute-start | bytes 98312 | tf_op jit(solution)/shard_map/ppermute | solution.py:25
  55.7 9.0 %collective-permute-start.2 = (bf16[2,32,256]{2,1,0:T(8,128)(2,1)S(1)}, bf16[2,32,256]{2,1,0:T(8,128)(2,1)S(1)}, u32[]{:S(2)}, u32[]{:S(2)}) collective-permute-start(bf16[2,32,256]{2,1,0:T(8,128)(2,1)S(1)} %get-tuple-element.326), channel_id=1, source_target_pairs={{64,0},{128,64},{192,128},{256,192},{320,256},{384,320},{448,384},... | collective-permute-start | bytes 98312 | tf_op jit(solution)/shard_map/ppermute | solution.py:25
  64.6 316.6 %reduce-scatter.12.cloned.1.call-start = ((), (), s32[]{:S(2)}) async-start(), calls=%async_computation.5 | async-start | bytes 278528
  66.7 315.4 %reduce-scatter.8.cloned.1.call-start = ((), (), s32[]{:S(2)}) async-start(), calls=%async_computation.3 | async-start | bytes 278528 | tf_op jit(solution)/shard_map/reduce_scatter | solution.py:119
Sparse Core Ops, SparseCore 0:
  64.7 60.9 reduce-scatter.9
  128.7 66.8 reduce-scatter.11
  198.3 66.6 reduce-scatter.7
where the time goes:
time: 570 us; the launch traced here: 569 us
  blocking collectives  489 us (86%)
  matrix products  28.9 us (5%)
  starting transfers between devices  18.8 us (3%)
  between operations  14 us (2%)
  other arithmetic  10.5 us (2%)
  local copies, waits for them, and re-layouts  6.95 us (1%)
    psum x1, blocking collectives, body(): geo_total = lax.psum(geo_local, ('slab', 'walker'))  310 us
    psum x1, blocking collectives, body(): lax.psum((partial_rows[0], partial_rows[1], partial_rows[2]), ('slab', 'g...  179 us
    dot_general x2, matrix products, walker_work(): jnp.einsum('bksm,bksf->bmf', onehot.astype(jnp.float32), d_pre.reshape(bl...  11.9 us
  transfers between devices with their start and end apart: 7, of which 0 were waited for; matrix products, arithmetic and copies ran while one was open for 2% of the time, Pallas kernels for 0%

commit v1 on v0

v1 whole, which is shorter than its diff:
```python
import functools

import jax
import jax.numpy as jnp
from jax import lax
from jax.experimental import pallas as pl
from jax.experimental.pallas import tpu as pltpu
from jax.sharding import PartitionSpec as P

RIM = 32
F32 = jnp.float32
BF16 = jnp.bfloat16
MESH = pl.DeviceIdType.MESH
BASES = (0, 8, 16, 24, 33, 41, 49, 57)
STEPS = 8


def dot(a, b, dims, **more):
    return lax.dot_general(a, b, (dims, ((), ())), preferred_element_type=F32, **more)


NN = ((1,), (0,))
NT = ((1,), (1,))
TN = ((0,), (0,))


def at(**coords):
    return dict(device_id=coords, device_id_type=MESH)


def halo_kernel(slabs, feats_ref, before_ref, after_ref, send_sem, recv_sem):
    me = lax.axis_index("slab")
    nxt, prv = lax.rem(me + 1, slabs), lax.rem(me + slabs - 1, slabs)
    barrier = pltpu.get_barrier_semaphore()
    pl.semaphore_signal(barrier, inc=1, **at(slab=nxt))
    pl.semaphore_signal(barrier, inc=1, **at(slab=prv))
    pl.semaphore_wait(barrier, 2)
    rows = feats_ref.shape[1]
    up = pltpu.make_async_remote_copy(
        feats_ref.at[:, pl.ds(rows - RIM, RIM)], before_ref, send_sem.at[0], recv_sem.at[0], **at(slab=nxt)
    )
    down = pltpu.make_async_remote_copy(
        feats_ref.at[:, pl.ds(0, RIM)], after_ref, send_sem.at[1], recv_sem.at[1], **at(slab=prv)
    )
    up.start()
    down.start()
    up.wait()
    down.wait()


def compute_kernel(
    lat_ref, feats_ref, before_ref, after_ref, ws_ref, wp_ref, wu_ref, geo_ref, nbr_ref, cnt_ref, env_ref, cot_ref,
    newf_ref, dp_ref, dq_ref, low_ref, high_ref, grads_ref, dgeo_ref,
    ext_ref, p_ref, q_ref, off_ref, wt_ref, w_ref, agg_ref, s_ref, d_ref, dqt_ref, t_ref,
):
    walkers, rows, width = feats_ref.shape
    slots = nbr_ref.shape[2]
    wide = q_ref.shape[1]
    lats = geo_ref.shape[0]
    lane = lax.broadcasted_iota(jnp.int32, (8, rows), 1)
    ws_t = ws_ref[...].T
    wp_t = wp_ref[...].T
    ext_ref[pl.ds(rows + 2 * RIM, wide - rows - 2 * RIM), :] = jnp.zeros((wide - rows - 2 * RIM, width), BF16)
    dgeo = jnp.zeros((lats, width), F32)
    for w in range(walkers):
        ext_ref[pl.ds(0, RIM), :] = before_ref[w]
        ext_ref[pl.ds(RIM, rows), :] = feats_ref[w]
        ext_ref[pl.ds(RIM + rows, RIM), :] = after_ref[w]
        ext_t = ext_ref[...].T
        feats_t = feats_ref[w].T
        lat = lat_ref[0, w]
        pick = (lax.broadcasted_iota(jnp.int32, (lats, rows), 0) == lat).astype(F32)
        p_t = dot(ws_t, feats_t, NN) + dot(geo_ref[...], pick, TN, precision=lax.Precision.HIGHEST)
        p_ref[...] = 0.5 * p_t
        q_ref[...] = 0.5 * dot(wp_t, ext_t, NN).astype(BF16).astype(F32)

        own = lax.broadcasted_iota(jnp.int32, (rows, slots), 0)
        rel = nbr_ref[w] - own
        rel = rel - (rel > RIM).astype(jnp.int32)
        off_ref[...] = rel.astype(F32).T.astype(jnp.int32)
        count = cnt_ref[pl.ds(w, 1), :]
        slot = lax.broadcasted_iota(jnp.int32, (slots, rows), 0)
        wt_ref[...] = jnp.where(slot < count, env_ref[w].astype(F32).T, 0.0)

        def place(step, acc):
            for u in range(8):
                k = step * 8 + u
                acc = acc + jnp.where(off_ref[pl.ds(k, 1), :] == slot, wt_ref[pl.ds(k, 1), :], 0.0)
            return acc

        weights = lax.fori_loop(0, slots // 8, place, jnp.zeros((slots, rows), F32))
        rolled = weights
        sub = lax.rem(slot, STEPS)
        for a in range(1, STEPS):
            rolled = jnp.where(sub == a, pltpu.roll(weights, a, 1), rolled)
        w_ref[...] = rolled

        def forward(tile, carry):
            r0 = pl.multiple_of(tile * 8, 8)
            p = p_ref[pl.ds(r0, 8), :]
            q = q_ref[pl.ds(r0, 8), :]
            qs = []
            for base in BASES:
                moved = q if base == 0 else pltpu.roll(q, wide - base, 1)
                qs.append((moved[:, :rows], moved[:, rows:]))
            agg = jnp.zeros((8, rows), F32)
            tot = jnp.zeros((8, rows), F32)
            for a in range(STEPS):
                pa = p if a == 0 else pltpu.roll(p, a, 1)
                ga = sa = None
                for b in range(len(BASES)):
                    m = b * STEPS + a
                    q0, q1 = qs[b]
                    h = pa + (q0 if a == 0 else jnp.where(lane < a, q1, q0))
                    u = 1.0 + jnp.tanh(h)
                    g = h * u
                    wm = w_ref[pl.ds(m, 1), :]
                    t = wm * (u + g * (2.0 - u))
                    t_ref[m, pl.ds(r0, 8), :] = t
                    ga = wm * g if ga is None else ga + wm * g
                    sa = t if sa is None else sa + t
                if a:
                    ga = pltpu.roll(ga, rows - a, 1)
                    sa = pltpu.roll(sa, rows - a, 1)
                agg = agg + ga
                tot = tot + sa
            agg_ref[pl.ds(r0, 8), :] = agg
            s_ref[pl.ds(r0, 8), :] = tot
            return carry

        lax.fori_loop(0, width // 8, forward, 0)

        inv = 1.0 / count.astype(F32)
        agg_t = (agg_ref[...] * inv).astype(BF16)
        upd = dot(agg_t.T, wu_ref[...], NN)
        sig = 0.5 + 0.5 * jnp.tanh(0.5 * upd)
        newf_ref[w] = (feats_ref[w].astype(F32) + upd * sig).astype(BF16)
        du = (cot_ref[w].astype(F32) * (sig * (1.0 + upd * (1.0 - sig)))).astype(BF16)
        dd = 0.5 * dot(wu_ref[...], du, NT) * inv
        d_ref[...] = dd
        dp = (dd * s_ref[...]).T
        dgeo = dgeo + jnp.where(
            lax.broadcasted_iota(jnp.int32, (lats, width), 0) == lat, jnp.sum(dp, axis=0, keepdims=True), 0.0
        )
        dp = dp.astype(BF16)
        dp_ref[w] = dp

        def backward(tile, carry):
            r0 = pl.multiple_of(tile * 8, 8)
            d = d_ref[pl.ds(r0, 8), :]
            nb = len(BASES)
            alls, wraps = [None] * nb, [None] * nb
            for a in range(STEPS):
                da = d if a == 0 else pltpu.roll(d, a, 1)
                for b in range(nb):
                    v = t_ref[b * STEPS + a, pl.ds(r0, 8), :] * da
                    alls[b] = v if a == 0 else alls[b] + v
                    if a:
                        c = jnp.where(lane < a, v, 0.0)
                        wraps[b] = c if a == 1 else wraps[b] + c
            out = jnp.zeros((8, wide), F32)
            for b, base in enumerate(BASES):
                both = jnp.concatenate((alls[b] - wraps[b], wraps[b]), axis=1)
                out = out + (both if base == 0 else pltpu.roll(both, base, 1))
            dqt_ref[pl.ds(r0, 8), :] = out
            return carry

        lax.fori_loop(0, width // 8, backward, 0)
        dq = dqt_ref[...].T
        dq_ref[w] = dq[RIM : RIM + rows]
        dqb = dq.astype(BF16)
        low_ref[w] = dqb[:RIM]
        high_ref[w] = dqb[RIM + rows : 2 * RIM + rows]
        terms = (dot(feats_t, dp, NN), dot(ext_t, dqb, NN), dot(agg_t, du, NN))
        for n in range(3):
            grads_ref[n] = terms[n] if w == 0 else grads_ref[n] + terms[n]
    dgeo_ref[...] = dgeo


def reduce_kernel(
    slabs, walks, geoms,
    grads_ref, low_ref, high_ref, dgeo_ref,
    out_ref, from_next_ref, from_prev_ref, geo_out_ref,
    core_out, core_in, half, plane_out, plane_in, ring_out, ring_in, gather_out, gather_in, gslab_in, gring_out, gring_in,
    send_sem, recv_sem,
):
    slab, z, geom = lax.axis_index("slab"), lax.axis_index("walker"), lax.axis_index("geom")
    core = lax.rem(geom, 2)
    pair = geom - core
    chips = slabs * geoms // 2
    chip = slab * (geoms // 2) + pair // 2
    nmat, rows, width = grads_ref.shape
    lanes = width // 2
    nxt, prv = lax.rem(slab + 1, slabs), lax.rem(slab + slabs - 1, slabs)

    def chip_at(c, k):
        return at(slab=c // (geoms // 2), geom=lax.rem(c, geoms // 2) * 2 + k)

    barrier = pltpu.get_barrier_semaphore()
    for k in range(2):
        kk = core if k == 0 else 1 - core
        for r in range(k ^ 1, chips):
            pl.semaphore_signal(barrier, inc=1, **chip_at(lax.rem(chip + r, chips), kk))
    for r in range(1, walks):
        pl.semaphore_signal(barrier, inc=1, **at(walker=lax.rem(z + r, walks)))
    pl.semaphore_wait(barrier, 2 * chips - 1 + walks - 1)

    def send(src, dst, n, where):
        c = pltpu.make_async_remote_copy(src, dst, send_sem.at[n], recv_sem.at[n], **where)
        c.start()
        return c

    def settle(ref, n):
        c = pltpu.make_async_remote_copy(ref, ref, send_sem.at[n], recv_sem.at[n], **at(slab=nxt))
        c.wait_send()
        c.wait_recv()

    down = send(low_ref, from_next_ref, 0, at(slab=prv))
    up = send(high_ref, from_prev_ref, 1, at(slab=nxt))

    mine = pl.ds(pl.multiple_of(core * lanes, lanes), lanes)
    theirs = pl.ds(pl.multiple_of((1 - core) * lanes, lanes), lanes)
    core_out[...] = grads_ref[:, :, theirs].astype(BF16)
    cross = send(core_out, core_in, 2, at(geom=pair + 1 - core))

    gslab_in[slab] = dgeo_ref[...]
    for r in range(1, slabs):
        send(dgeo_ref, gslab_in.at[slab], 3, at(slab=lax.rem(slab + r, slabs)))

    cross.wait()
    half[...] = grads_ref[:, :, mine] + core_in[...].astype(F32)

    for c in range(chips):
        for n in range(nmat):
            plane_out[c, n] = half[n, pl.ds(c, walks, stride=chips), :].astype(BF16)
    plane_in[chip] = plane_out[chip]
    for r in range(1, chips):
        to = lax.rem(chip + r, chips)
        send(plane_out.at[to], plane_in.at[chip], 4, chip_at(to, core))

    settle(gslab_in.at[pl.ds(0, slabs - 1)], 3)
    gsum = gslab_in[0]
    for s in range(1, slabs):
        gsum = gsum + gslab_in[s]
    gring_out[...] = gsum
    gring_in[z] = gsum
    for r in range(1, walks):
        send(gring_out, gring_in.at[z], 5, at(walker=lax.rem(z + r, walks)))

    settle(plane_in.at[pl.ds(0, chips - 1)], 4)
    part = plane_in[0].astype(F32)
    for c in range(1, chips):
        part = part + plane_in[c].astype(F32)

    ring_out[...] = jnp.zeros(ring_out.shape, F32)
    for n in range(nmat):
        for v in range(walks):
            ring_out[v, pl.ds(n, 1), :] = part[n, v : v + 1, :]
    ring_in[z] = ring_out[z]
    for r in range(1, walks):
        to = lax.rem(z + r, walks)
        send(ring_out.at[to], ring_in.at[z], 6, at(walker=to))
    settle(ring_in.at[pl.ds(0, walks - 1)], 6)
    row = ring_in[0]
    for v in range(1, walks):
        row = row + ring_in[v]

    slot = core * chips + chip
    gather_out[...] = row
    gather_in[slot] = row
    for k in range(2):
        kk = core if k == 0 else 1 - core
        for r in range(k ^ 1, chips):
            send(gather_out, gather_in.at[slot], 7, chip_at(lax.rem(chip + r, chips), kk))

    settle(gring_in.at[pl.ds(0, walks - 1)], 5)
    gsum = gring_in[0]
    for v in range(1, walks):
        gsum = gsum + gring_in[v]
    geo_out_ref[...] = gsum

    settle(gather_in.at[pl.ds(0, 2 * chips - 1)], 7)
    for n in range(nmat):
        for k in range(2):
            for c in range(chips):
                out_ref[n, pl.ds(c, 1), pl.ds(k * lanes, lanes)] = gather_in[k * chips + c, pl.ds(n, 1), :]
    down.wait()
    up.wait()


def finish_kernel(cot_ref, dp_ref, dq_ref, from_next_ref, from_prev_ref, ws_ref, wp_ref, grads_ref, geo_ref,
                  df_ref, gs_ref, gp_ref, gu_ref, geo_out_ref):
    walkers, rows, width = dq_ref.shape
    for w in range(walkers):
        dq = jnp.concatenate(
            (
                dq_ref[w, pl.ds(0, RIM), :] + from_prev_ref[w].astype(F32),
                dq_ref[w, pl.ds(RIM, rows - 2 * RIM), :],
                dq_ref[w, pl.ds(rows - RIM, RIM), :] + from_next_ref[w].astype(F32),
            ),
            axis=0,
        ).astype(BF16)
        df_ref[w] = cot_ref[w].astype(F32) + dot(dp_ref[w], ws_ref[...], NT) + dot(dq, wp_ref[...], NT)
    gs_ref[...] = grads_ref[0]
    gp_ref[...] = grads_ref[1]
    gu_ref[...] = grads_ref[2]
    geo_out_ref[...] = geo_ref[...]


def vmem(n):
    return [pl.BlockSpec(memory_space=pltpu.VMEM)] * n


def body(sizes, features, w_self, w_pair, w_update, geo_embed, lattice, neighbours, counts, envelope, cotangent):
    slabs, walks, geoms = sizes
    feats, cot = features[0], cotangent[0]
    walkers, rows, width = feats.shape
    slots = neighbours.shape[3]
    lats = geo_embed.shape[1]
    wide = 2 * rows
    sds = jax.ShapeDtypeStruct
    rim = sds((walkers, RIM, width), BF16)
    before, after = pl.pallas_call(
        functools.partial(halo_kernel, slabs),
        out_shape=(rim, rim),
        in_specs=vmem(1),
        out_specs=vmem(2),
        scratch_shapes=[pltpu.SemaphoreType.DMA((2,)), pltpu.SemaphoreType.DMA((2,))],
        compiler_params=pltpu.CompilerParams(collective_id=0, has_side_effects=True),
        name="halo",
    )(feats)

    newf, dp, dq, low, high, grads, dgeo = pl.pallas_call(
        compute_kernel,
        out_shape=(
            sds((walkers, rows, width), BF16),
            sds((walkers, rows, width), BF16),
            sds((walkers, rows, width), F32),
            rim,
            rim,
            sds((3, width, width), F32),
            sds((lats, width), F32),
        ),
        in_specs=[pl.BlockSpec(memory_space=pltpu.SMEM)] + vmem(11),
        out_specs=vmem(7),
        scratch_shapes=[
            pltpu.VMEM((wide, width), BF16),
            pltpu.VMEM((width, rows), F32),
            pltpu.VMEM((width, wide), F32),
            pltpu.VMEM((slots, rows), jnp.int32),
            pltpu.VMEM((slots, rows), F32),
            pltpu.VMEM((slots, rows), F32),
            pltpu.VMEM((width, rows), F32),
            pltpu.VMEM((width, rows), F32),
            pltpu.VMEM((width, rows), F32),
            pltpu.VMEM((width, wide), F32),
            pltpu.VMEM((slots, width, rows), F32),
        ],
        compiler_params=pltpu.CompilerParams(vmem_limit_bytes=40 * 1024 * 1024),
        name="compute",
    )(lattice, feats, before, after, w_self, w_pair, w_update, geo_embed[0], neighbours[0], counts[0], envelope[0], cot)

    chips = slabs * geoms // 2
    lanes = width // 2
    gsum, from_next, from_prev, geo = pl.pallas_call(
        functools.partial(reduce_kernel, slabs, walks, geoms),
        out_shape=(sds((3, width // walks, width), F32), rim, rim, sds((lats, width), F32)),
        in_specs=vmem(4),
        out_specs=vmem(4),
        scratch_shapes=[
            pltpu.VMEM((3, width, lanes), BF16),
            pltpu.VMEM((3, width, lanes), BF16),
            pltpu.VMEM((3, width, lanes), F32),
            pltpu.VMEM((chips, 3, walks, lanes), BF16),
            pltpu.VMEM((chips, 3, walks, lanes), BF16),
            pltpu.VMEM((walks, 8, lanes), F32),
            pltpu.VMEM((walks, 8, lanes), F32),
            pltpu.VMEM((8, lanes), F32),
            pltpu.VMEM((2 * chips, 8, lanes), F32),
            pltpu.VMEM((slabs, lats, width), F32),
            pltpu.VMEM((lats, width), F32),
            pltpu.VMEM((walks, lats, width), F32),
            pltpu.SemaphoreType.DMA((8,)),
            pltpu.SemaphoreType.DMA((8,)),
        ],
        compiler_params=pltpu.CompilerParams(
            collective_id=1, has_side_effects=True, vmem_limit_bytes=16 * 1024 * 1024
        ),
        name="reduce",
    )(grads, low, high, dgeo)

    share = sds((width // walks, width), F32)
    dfeats, gs, gp, gu, dgeo_all = pl.pallas_call(
        finish_kernel,
        out_shape=(sds((walkers, rows, width), F32), share, share, share, sds((lats, width), F32)),
        in_specs=vmem(9),
        out_specs=vmem(5),
        name="finish",
    )(cot, dp, dq, from_next, from_prev, w_self, w_pair, gsum, geo)
    return newf[None], dfeats[None], gs, gp, gu, dgeo_all[None]


def solution(mesh):
    sizes = (mesh.shape["slab"], mesh.shape["walker"], mesh.shape["geom"])
    return jax.shard_map(
        functools.partial(body, sizes),
        mesh=mesh,
        in_specs=(
            P("geom", "walker", "slab", None),
            P(),
            P(),
            P(),
            P("geom", None, None),
            P("geom", "walker"),
            P("geom", "walker", "slab", None),
            P("geom", "walker", "slab"),
            P("geom", "walker", "slab", None),
            P("geom", "walker", "slab", None),
        ),
        out_specs=(
            P("geom", "walker", "slab", None),
            P("geom", "walker", "slab", None),
            P("walker", None),
            P("walker", None),
            P("walker", None),
            P("geom", None, None),
        ),
        check_vma=False,
    )
```

time: 570 us -> 87.5 us (0.15)
  blocking collectives: 489 us -> 0 us
  Pallas kernels: 0 us -> 78.8 us
  matrix products: 28.9 us -> 0 us
  starting transfers between devices: 18.8 us -> 0 us
  between operations: 14 us -> 0.79 us
  other arithmetic: 10.5 us -> 0 us
    psum x2 -> x0, blocking collectives: 489 us -> none  [the longest x1 310 us: body(): geo_total = lax.psum(geo_local, ('slab', 'walker'))]
    pallas_call x0 -> x4, Pallas kernels: none -> 78.8 us  [the longest x1 36.1 us: body(): pl.pallas_call(functools.partial(reduce_kernel, slabs, walks, geoms), out...]
    dot_general x17 -> x0, matrix products: 28.9 us -> none  [the longest x2 11.9 us: walker_work(): jnp.einsum('bksm,bksf->bmf', onehot.astype(jnp.float32), d_pre.reshape(bl...]
    ppermute x4 -> x0, starting transfers between devices: 18.7 us -> none  [the longest x2 8.9 us: shifted(): return lax.ppermute(block, axis, route)]
    reduce_sum x3 -> x0, other arithmetic: 8.24 us -> none  [the longest x2 8.2 us: walker_work(): d_self = jnp.sum(d_pre, axis=1)]
  transfers between devices with their start and end apart: 7 -> 0, of which waited for: 0 -> 0; matrix products, arithmetic and copies ran while one was open for 2% -> 0% of each run, Pallas kernels for 0% -> 0%
where the time goes in v1:
time: 87.5 us; the launch traced here: 87.1 us
  Pallas kernels  78.8 us (90%)
  local copies, waits for them, and re-layouts  7.52 us (9%)
    pallas_call x1, Pallas kernels, body(): pl.pallas_call(functools.partial(reduce_kernel, slabs, walks, geoms), out...  36.1 us
    pallas_call x1, Pallas kernels, body(): pl.pallas_call(compute_kernel, out_shape=(sds((walkers, rows, width), BF1...  30.3 us
    pallas_call x1, Pallas kernels, body(): pl.pallas_call(functools.partial(halo_kernel, slabs), out_shape=(rim, rim...  10.2 us
    unnamed x34, local copies, waits for them, and re-layouts  7.52 us
    pallas_call x1, Pallas kernels, body(): pl.pallas_call(finish_kernel, out_shape=(sds((walkers, rows, width), F32)...  2.25 us

profile of v1, /device:TPU:1, one launch (start us, length us, event | category | flops | bytes accessed | tf_op | source)
XLA Modules:
  0.0 87.1 jit_solution(6954314808937142837)
XLA Ops:
  0.6 0.0 copy-start.2
  0.6 0.9 %copy.17 = bf16[1,2,128,64]{3,2,1,0:T(8,128)(2,1)S(1)} copy(bf16[1,2,128,64]{2,3,1,0:T(8,128)(2,1)} %param.18) | data formatting | bytes 65536 | tf_op args[8]
  1.6 0.0 copy-start.1
  1.6 10.2 %halo.1 = (bf16[2,32,256]{2,1,0:T(8,128)(2,1)}, bf16[2,32,256]{2,1,0:T(8,128)(2,1)}) custom-call(bf16[2,128,256]{2,1,0:T(8,128)(2,1)} %bitcast.11), custom_call_target="tpu_custom_call" | custom-call | tf_op jit(solution)/shard_map/halo/pallas_call | solution.py:323
  11.8 0.0 copy-start
  11.8 0.0 copy-start.10
  11.8 0.0 copy-start.12
  11.8 1.0 %copy.16 = s32[1,2,128,64]{3,2,1,0:T(8,128)S(1)} copy(s32[1,2,128,64]{2,3,1,0:T(8,128)} %param.16) | data formatting | bytes 131072 | tf_op args[6]
  12.8 0.0 copy-start.14
  12.8 0.0 copy-start.15
  12.8 0.0 copy-done.2
  12.8 0.0 copy-done.1
  12.8 0.0 copy-done
  12.8 0.0 copy-done.10
  12.9 0.0 copy-done.12
  12.9 0.6 copy-done.14
  13.5 0.0 copy-done.15
  13.5 0.0 copy-start.3
  13.5 0.9 %copy-done.3 = bf16[1,2,128,256]{3,2,1,0:T(8,128)(2,1)S(1)} copy-done((bf16[1,2,128,256]{3,2,1,0:T(8,128)(2,1)S(1)}, bf16[1,2,128,256]{3,2,1,0:T(8,128)(2,1)}, u32[]{:S(2)}) %copy-start.3) | copy-done | bytes 131096
  14.4 0.0 copy-start.6
  14.4 0.9 %copy-done.6 = bf16[256,256]{1,0:T(8,128)(2,1)S(1)} copy-done((bf16[256,256]{1,0:T(8,128)(2,1)S(1)}, bf16[256,256]{1,0:T(8,128)(2,1)}, u32[]{:S(2)}) %copy-start.6) | copy-done | bytes 131096
  15.3 0.0 copy-start.11
  15.3 0.8 copy-done.11
  16.0 30.3 %compute.1 = (bf16[2,128,256]{2,1,0:T(8,128)(2,1)}, bf16[2,128,256]{2,1,0:T(8,128)(2,1)S(1)}, f32[2,128,256]{2,1,0:T(8,128)S(1)}, bf16[2,32,256]{2,1,0:T(8,128)(...) custom-call(s32[1,2]{1,0:T(1,128)S(1)} %copy-done.15, ...), custom_call_target="tpu_custom_call" | custom-call | tf_op jit(solution)/shard_map/compute/pallas_call | solution.py:333
  46.4 0.0 copy-start.4
  46.4 0.0 copy-start.5
  46.4 36.1 %reduce.1 = (f32[3,16,256]{2,1,0:T(8,128)S(1)}, bf16[2,32,256]{2,1,0:T(8,128)(2,1)S(1)}, bf16[2,32,256]{2,1,0:T(8,128)(2,1)S(1)}, f32[2,256]{1,0:T(2,128)S(1)}) custom-call(f32[3,256,256]{2,1,0:T(8,128)S(1)} %get-tuple-element.29.grads_ref, bf16[2,32,256]{2,1,0:T(8,128)(2,1)S(1)} %get-tuple-element.30.low_ref, ...), custom_call_target="tpu_custom_call" | custom-call | tf_op jit(solution)/shard_map/reduce/pallas_call | solution.py:365
  82.5 0.0 copy-done.4
  82.5 0.0 copy-done.5
  82.5 0.0 copy-start.7
  82.5 0.6 copy-done.7
  83.1 0.0 copy-start.8
  83.1 0.6 copy-done.8
  83.7 0.0 copy-start.9
  83.7 0.6 copy-done.9
  84.3 0.0 copy-start.13
  84.3 0.6 copy-done.13
  84.9 2.3 %finish.1 = (f32[2,128,256]{2,1,0:T(8,128)}, f32[16,256]{1,0:T(8,128)}, f32[16,256]{1,0:T(8,128)}, f32[16,256]{1,0:T(8,128)}, f32[2,256]{1,0:T(2,128)}) custom-call(bf16[2,128,256]{2,1,0:T(8,128)(2,1)} %bitcast.9, bf16[2,128,256]{2,1,0:T(8,128)(2,1)} %copy-done.5, f32[2,128,256]{2,1,0:T(8,128)} %copy-done.4, bf16[2,32,256]{2,1,0:T(8,128)(2,1)} %copy-done.8, ...), custom_call_target="tpu_custom_call" | custom-call | tf_op jit(solution)/shard_map/finish/pallas_call | solution.py:393
Async XLA Ops:
  0.6 12.2 %copy-start.2 = (bf16[1,2,128,256]{3,2,1,0:T(8,128)(2,1)S(1)}, bf16[1,2,128,256]{3,2,1,0:T(8,128)(2,1)}, u32[]{:S(2)}) copy-start(bf16[1,2,128,256]{3,2,1,0:T(8,128)(2,1)} %param.19) | copy-start | bytes 393220
  1.6 11.3 %copy-start.1 = (bf16[256,256]{1,0:T(8,128)(2,1)S(1)}, bf16[256,256]{1,0:T(8,128)(2,1)}, u32[]{:S(2)}) copy-start(bf16[256,256]{1,0:T(8,128)(2,1)} %wp_ref.3) | copy-start | bytes 393220
  11.8 1.1 %copy-start = (bf16[256,256]{1,0:T(8,128)(2,1)S(1)}, bf16[256,256]{1,0:T(8,128)(2,1)}, u32[]{:S(2)}) copy-start(bf16[256,256]{1,0:T(8,128)(2,1)} %ws_ref.3) | copy-start | bytes 393220
  11.8 1.1 %copy-start.10 = (bf16[2,32,256]{2,1,0:T(8,128)(2,1)S(1)}, bf16[2,32,256]{2,1,0:T(8,128)(2,1)}, u32[]{:S(2)}) copy-start(bf16[2,32,256]{2,1,0:T(8,128)(2,1)} %get-tuple-element.24.before_ref) | copy-start | bytes 98308
  11.8 1.1 %copy-start.12 = (f32[1,2,256]{2,1,0:T(2,128)S(1)}, f32[1,2,256]{2,1,0:T(2,128)}, u32[]{:S(2)}) copy-start(f32[1,2,256]{2,1,0:T(2,128)} %param.14) | copy-start | bytes 6148
  12.8 0.7 copy-start.14
  12.8 0.7 copy-start.15
  13.5 0.9 %copy-start.3 = (bf16[1,2,128,256]{3,2,1,0:T(8,128)(2,1)S(1)}, bf16[1,2,128,256]{3,2,1,0:T(8,128)(2,1)}, u32[]{:S(2)}) copy-start(bf16[1,2,128,256]{3,2,1,0:T(8,128)(2,1)} %param.10) | copy-start | bytes 393220
  14.4 0.9 %copy-start.6 = (bf16[256,256]{1,0:T(8,128)(2,1)S(1)}, bf16[256,256]{1,0:T(8,128)(2,1)}, u32[]{:S(2)}) copy-start(bf16[256,256]{1,0:T(8,128)(2,1)} %wu_ref.1) | copy-start | bytes 393220
  15.3 0.8 copy-start.11
  46.4 36.1 %copy-start.4 = (f32[2,128,256]{2,1,0:T(8,128)}, f32[2,128,256]{2,1,0:T(8,128)S(1)}, u32[]{:S(2)}) copy-start(f32[2,128,256]{2,1,0:T(8,128)S(1)} %get-tuple-element.28.dq_ref) | copy-start | bytes 786436
  46.4 36.1 %copy-start.5 = (bf16[2,128,256]{2,1,0:T(8,128)(2,1)}, bf16[2,128,256]{2,1,0:T(8,128)(2,1)S(1)}, u32[]{:S(2)}) copy-start(bf16[2,128,256]{2,1,0:T(8,128)(2,1)S(1)} %get-tuple-element.27.dp_ref) | copy-start | bytes 393220
  82.5 0.6 copy-start.7
  83.1 0.6 copy-start.8
  83.7 0.6 copy-start.9
  84.3 0.6 copy-start.13

commit v2 on v0

v2 whole, which is shorter than its diff:
```python
import functools

import jax
import jax.numpy as jnp
from jax import lax
from jax.experimental import pallas as pl
from jax.experimental.pallas import tpu as pltpu
from jax.sharding import PartitionSpec as P

RIM = 32
F32 = jnp.float32
BF16 = jnp.bfloat16
MESH = pl.DeviceIdType.MESH
BASES = (0, 8, 16, 24, 33, 41, 49, 57)
STEPS = 8
TILE = 16
MIB = 1024 * 1024
NN = ((1,), (0,))
NT = ((1,), (1,))


def dot(a, b, dims):
    return lax.dot_general(a, b, (dims, ((), ())), preferred_element_type=F32)


def split_dot(a, b, dims):
    high = a.astype(BF16)
    return dot(high, b, dims) + dot((a - high.astype(F32)).astype(BF16), b, dims)


def at(**coords):
    return dict(device_id=coords, device_id_type=MESH)


def iota(shape, dim):
    return lax.broadcasted_iota(jnp.int32, shape, dim)


def shift_matrices(turn_ref, slide_ref):
    rows = turn_ref.shape[0]
    wide = slide_ref.shape[0]
    for a in range(STEPS):
        moved = lax.rem(iota((rows, rows), 0) + a, rows)
        turn_ref[:, a * rows : (a + 1) * rows] = (moved == iota((rows, rows), 1)).astype(F32).astype(BF16)
    for b, base in enumerate(BASES):
        moved = iota((wide, wide), 1) + base
        slide_ref[:, b * wide : (b + 1) * wide] = (moved == iota((wide, wide), 0)).astype(F32).astype(BF16)


def slot_weights(nbr, env, count, off_ref, wt_ref):
    slots, rows = nbr.shape
    rel = nbr - iota((slots, rows), 1)
    off_ref[...] = rel - (rel > RIM).astype(jnp.int32)
    slot = iota((slots, rows), 0)
    wt_ref[...] = jnp.where(slot < count, env.astype(F32), 0.0)

    def place(step, acc):
        for u in range(8):
            k = step * 8 + u
            acc = acc + jnp.where(off_ref[pl.ds(k, 1), :] == slot, wt_ref[pl.ds(k, 1), :], 0.0)
        return acc

    weights = lax.fori_loop(0, slots // 8, place, jnp.zeros((slots, rows), F32))
    turned = weights
    sub = lax.rem(slot, STEPS)
    for a in range(1, STEPS):
        turned = jnp.where(sub == a, pltpu.roll(weights, a, 1), turned)
    return turned


def forward_pass(walkers, p_ref, q_ref, w_ref, t_ref, agg_ref, tot_ref):
    rows = w_ref.shape[2]
    tiles = p_ref.shape[0] // TILE
    lane = iota((TILE, rows), 1)

    def tile_work(tile, carry):
        r0 = pl.multiple_of(tile * TILE, TILE)
        w = tile // (tiles // walkers)
        here = pl.ds(r0, TILE)
        for a in range(STEPS):
            pa = p_ref[here, a * rows : (a + 1) * rows]
            ga, sa = [], []
            for b in range(len(BASES)):
                m = b * STEPS + a
                h = q_ref[here, 2 * b * rows : (2 * b + 1) * rows]
                if a:
                    h = jnp.where(lane < a, q_ref[here, (2 * b + 1) * rows : (2 * b + 2) * rows], h)
                h = h + pa
                u = 1.0 + jnp.tanh(h)
                g = h * u
                wm = w_ref[w, pl.ds(m, 1), :]
                t = wm * (u + g * (2.0 - u))
                t_ref[m, here, :] = t
                ga.append(wm * g)
                sa.append(t)
            while len(ga) > 1:
                ga = [ga[n] + ga[n + 1] for n in range(0, len(ga), 2)]
                sa = [sa[n] + sa[n + 1] for n in range(0, len(sa), 2)]
            agg_ref[here, a * rows : (a + 1) * rows] = ga[0].astype(BF16)
            tot_ref[here, a * rows : (a + 1) * rows] = sa[0].astype(BF16)
        return carry

    lax.fori_loop(0, tiles, tile_work, 0)


def backward_pass(first, count, d_ref, t_ref, v_ref):
    rows = t_ref.shape[2]
    nb = len(BASES)
    lane = iota((TILE, rows), 1)

    def tile_work(tile, carry):
        here = pl.ds(pl.multiple_of(tile * TILE, TILE), TILE)
        ds = [d_ref[here, a * rows : (a + 1) * rows] for a in range(STEPS)]
        for b in range(nb):
            total = wrap = None
            for a in range(STEPS):
                v = t_ref[b * STEPS + a, here, :] * ds[a]
                total = v if a == 0 else total + v
                if a:
                    c = jnp.where(lane < a, v, 0.0)
                    wrap = c if a == 1 else wrap + c
            v_ref[here, 2 * b * rows : (2 * b + 1) * rows] = (total - wrap).astype(BF16)
            v_ref[here, (2 * b + 1) * rows : (2 * b + 2) * rows] = wrap.astype(BF16)
        return carry

    lax.fori_loop(first, first + count, tile_work, 0)


def first_kernel(
    slabs, lat_ref, feats_hbm, nbr_hbm, env_hbm, cnt_hbm, ws_hbm, geo_hbm,
    before_ref, after_ref, w_ref, p_ref, turn_ref, slide_ref, feats_ref,
    nbr_ref, env_ref, cnt_ref, ws_ref, geo_ref, off_ref, wt_ref, load_sem, send_sem, recv_sem,
):
    me = lax.axis_index("slab")
    nxt, prv = lax.rem(me + 1, slabs), lax.rem(me + slabs - 1, slabs)
    barrier = pltpu.get_barrier_semaphore()
    pl.semaphore_signal(barrier, inc=1, **at(slab=nxt))
    pl.semaphore_signal(barrier, inc=1, **at(slab=prv))
    loads = []
    for n, (src, dst) in enumerate((
        (feats_hbm, feats_ref), (nbr_hbm, nbr_ref), (env_hbm, env_ref), (cnt_hbm, cnt_ref), (ws_hbm, ws_ref), (geo_hbm, geo_ref),
    )):
        loads.append(pltpu.make_async_copy(src, dst, load_sem.at[n]))
        loads[-1].start()
    walkers, rows, width = feats_ref.shape
    shift_matrices(turn_ref, slide_ref)
    for c in loads:
        c.wait()
    pl.semaphore_wait(barrier, 2)
    up = pltpu.make_async_remote_copy(
        feats_ref.at[:, pl.ds(rows - RIM, RIM)], before_ref, send_sem.at[0], recv_sem.at[0], **at(slab=nxt)
    )
    down = pltpu.make_async_remote_copy(
        feats_ref.at[:, pl.ds(0, RIM)], after_ref, send_sem.at[1], recv_sem.at[1], **at(slab=prv)
    )
    up.start()
    down.start()
    ws_t = ws_ref[...].T
    geo = geo_ref[...]
    for w in range(walkers):
        w_ref[w] = slot_weights(nbr_ref[w], env_ref[w], cnt_ref[pl.ds(w, 1), :], off_ref, wt_ref)
        lats = geo.shape[0]
        row = jnp.sum(jnp.where(iota((lats, width), 0) == lat_ref[0, w], geo, 0.0), axis=0, keepdims=True)
        p = (dot(feats_ref[w], ws_ref[...], NN) + row).T
        p_ref[w * width : (w + 1) * width, :] = split_dot(0.5 * p, turn_ref[...], NN)
    up.wait()
    down.wait()


def main_kernel(
    slabs, walks, geoms,
    lat_ref, cnt_ref, before_ref, after_ref, w_ref, p_ref, turn_ref, slide_ref, feats_ref, ws_hbm, wp_hbm, wu_hbm, cot_hbm,
    newf_ref, df_ref, share_ref, geo_out_ref,
    ws_ref, wp_ref, wu_ref, cot_ref, ext_ref, ext_t_ref, q_ref, t_ref, agg_ref, tot_ref, d_ref, v_ref, own_ref,
    rim_out, rim_in, grads_ref, half_us, half_p,
    core_out_us, core_in_us, core_out_p, core_in_p, plane_out, plane_in, ring_out_us, ring_in_us, ring_out_p, ring_in_p,
    row_us, gather_us, row_p, gather_p, gslab_out, gslab_in, gring_out, gring_in,
    load_sem, send_sem, recv_sem,
):
    slab, z, geom = lax.axis_index("slab"), lax.axis_index("walker"), lax.axis_index("geom")
    core = lax.rem(geom, 2)
    pair = geom - core
    half_geoms = geoms // 2
    chips = slabs * half_geoms
    chip = slab * half_geoms + pair // 2
    nxt, prv = lax.rem(slab + 1, slabs), lax.rem(slab + slabs - 1, slabs)
    walkers, rows, width = feats_ref.shape
    lanes = width // 2
    lats = gslab_out.shape[0]
    tiles = walkers * width // TILE

    def chip_at(c, k):
        return at(slab=c // half_geoms, geom=lax.rem(c, half_geoms) * 2 + k)

    barrier = pltpu.get_barrier_semaphore()
    for k in range(2):
        kk = core if k == 0 else 1 - core
        for r in range(k ^ 1, chips):
            pl.semaphore_signal(barrier, inc=1, **chip_at(lax.rem(chip + r, chips), kk))
    for r in range(1, walks):
        pl.semaphore_signal(barrier, inc=1, **at(walker=lax.rem(z + r, walks)))

    def send(src, dst, n, where):
        c = pltpu.make_async_remote_copy(src, dst, send_sem.at[n], recv_sem.at[n], **where)
        c.start()
        return c

    def settle(ref, n):
        c = pltpu.make_async_remote_copy(ref, ref, send_sem.at[n], recv_sem.at[n], **at(slab=nxt))
        c.wait_send()
        c.wait_recv()

    loads = []
    for n, (src, dst) in enumerate(((wp_hbm, wp_ref), (wu_hbm, wu_ref), (cot_hbm, cot_ref), (ws_hbm, ws_ref))):
        loads.append(pltpu.make_async_copy(src, dst, load_sem.at[n]))
        loads[-1].start()

    wide = ext_ref.shape[1]
    for w in range(walkers):
        ext_ref[w, pl.ds(0, RIM), :] = before_ref[w]
        ext_ref[w, pl.ds(RIM, rows), :] = feats_ref[w]
        ext_ref[w, pl.ds(RIM + rows, RIM), :] = after_ref[w]
        ext_ref[w, pl.ds(2 * RIM + rows, wide - rows - 2 * RIM), :] = jnp.zeros((wide - rows - 2 * RIM, width), BF16)
    for c in loads:
        c.wait()
    for w in range(walkers):
        q = (0.5 * dot(ext_ref[w], wp_ref[...], NN)).astype(BF16)
        ext_t_ref[w] = ext_ref[w].T
        q_ref[w * width : (w + 1) * width, :] = dot(q.T, slide_ref[...], NN)

    forward_pass(walkers, p_ref, q_ref, w_ref, t_ref, agg_ref, tot_ref)

    dgeo = jnp.zeros((lats, width), F32)
    dps = []
    for w in range(walkers):
        part = slice(w * width, (w + 1) * width)
        inv = 1.0 / cnt_ref[pl.ds(w, 1), :].astype(F32)
        agg_t = (dot(agg_ref[part, :], turn_ref[...], NT) * inv).astype(BF16)
        upd = dot(agg_t.T, wu_ref[...], NN)
        sig = 0.5 + 0.5 * jnp.tanh(0.5 * upd)
        newf_ref[w] = (feats_ref[w].astype(F32) + upd * sig).astype(BF16)
        du = (cot_ref[w].astype(F32) * (sig * (1.0 + upd * (1.0 - sig)))).astype(BF16)
        dd = 0.5 * dot(wu_ref[...], du, NT) * inv
        d_ref[part, :] = split_dot(dd, turn_ref[...], NN)
        dp = (dd * dot(tot_ref[part, :], turn_ref[...], NT)).T
        mine = iota((lats, width), 0) == lat_ref[0, w]
        dgeo = dgeo + jnp.where(mine, jnp.sum(dp, axis=0, keepdims=True), 0.0)
        dp = dp.astype(BF16)
        dps.append(dp)
        feats_t = feats_ref[w].T
        for n, term in enumerate((dot(feats_t, dp, NN), dot(agg_t, du, NN))):
            grads_ref[n] = term if w == 0 else grads_ref[n] + term
    gslab_out[...] = dgeo
    for w in range(walkers):
        df_ref[w] = cot_ref[w].astype(F32) + dot(dps[w], ws_ref[...], NT)

    mine = pl.ds(pl.multiple_of(core * lanes, lanes), lanes)
    theirs = pl.ds(pl.multiple_of((1 - core) * lanes, lanes), lanes)
    core_out_us[...] = grads_ref[pl.ds(0, 2), :, theirs].astype(BF16)
    pl.semaphore_wait(barrier, 2 * chips - 1 + walks - 1)
    cross = send(core_out_us, core_in_us, 0, at(geom=pair + 1 - core))
    gslab_in[slab] = gslab_out[...]
    for r in range(1, slabs):
        send(gslab_out, gslab_in.at[slab], 1, at(slab=lax.rem(slab + r, slabs)))

    backward_pass(0, tiles // 2, d_ref, t_ref, v_ref)

    cross.wait()
    half_us[...] = grads_ref[pl.ds(0, 2), :, mine] + core_in_us[...].astype(F32)
    for c in range(chips):
        for n in range(2):
            plane_out[c, n] = half_us[n, pl.ds(c, walks, stride=chips), :].astype(BF16)
    plane_in[chip] = plane_out[chip]
    for r in range(1, chips):
        to = lax.rem(chip + r, chips)
        send(plane_out.at[to], plane_in.at[chip], 2, chip_at(to, core))

    backward_pass(tiles // 2, tiles // 2, d_ref, t_ref, v_ref)

    for w in range(walkers):
        dq = dot(v_ref[w * width : (w + 1) * width, :], slide_ref[...], NT).T
        own_ref[w] = dq[RIM : RIM + rows]
        dqb = dq.astype(BF16)
        rim_out[0, w] = dqb[:RIM]
        rim_out[1, w] = dqb[RIM + rows : 2 * RIM + rows]
        term = dot(ext_t_ref[w], dqb, NN)
        grads_ref[2] = term if w == 0 else grads_ref[2] + term
    core_out_p[...] = grads_ref[2, :, theirs].astype(BF16)
    cross = send(core_out_p, core_in_p, 3, at(geom=pair + 1 - core))
    down = send(rim_out.at[0], rim_in.at[0], 4, at(slab=prv))
    up = send(rim_out.at[1], rim_in.at[1], 5, at(slab=nxt))
    cross.wait()
    half_p[...] = (grads_ref[2, :, mine] + core_in_p[...].astype(F32)).astype(BF16)
    for v in range(walks):
        ring_out_p[v] = half_p[pl.ds(v * (width // walks), width // walks), :]
    ring_in_p[z] = ring_out_p[z]
    for r in range(1, walks):
        to = lax.rem(z + r, walks)
        send(ring_out_p.at[to], ring_in_p.at[z], 6, at(walker=to))

    settle(gslab_in.at[pl.ds(0, slabs - 1)], 1)
    gsum = gslab_in[0]
    for s in range(1, slabs):
        gsum = gsum + gslab_in[s]
    gring_out[...] = gsum
    gring_in[z] = gsum
    for r in range(1, walks):
        send(gring_out, gring_in.at[z], 7, at(walker=lax.rem(z + r, walks)))

    settle(plane_in.at[pl.ds(0, chips - 1)], 2)
    part = plane_in[0].astype(F32)
    for c in range(1, chips):
        part = part + plane_in[c].astype(F32)
    for v in range(walks):
        for n in range(2):
            ring_out_us[v, pl.ds(n, 1), :] = part[n, v : v + 1, :]
    ring_in_us[z] = ring_out_us[z]
    for r in range(1, walks):
        to = lax.rem(z + r, walks)
        send(ring_out_us.at[to], ring_in_us.at[z], 8, at(walker=to))

    down.wait()
    up.wait()
    for w in range(walkers):
        dq = jnp.concatenate(
            (
                own_ref[w, pl.ds(0, RIM), :] + rim_in[1, w].astype(F32),
                own_ref[w, pl.ds(RIM, rows - 2 * RIM), :],
                own_ref[w, pl.ds(rows - RIM, RIM), :] + rim_in[0, w].astype(F32),
            ),
            axis=0,
        ).astype(BF16)
        df_ref[w] = df_ref[w] + dot(dq, wp_ref[...], NT)

    slot = core * chips + chip
    settle(ring_in_p.at[pl.ds(0, walks - 1)], 6)
    part = ring_in_p[0].astype(F32)
    for v in range(1, walks):
        part = part + ring_in_p[v].astype(F32)
    row_p[...] = part.astype(BF16)
    gather_p[slot] = row_p[...]
    for k in range(2):
        kk = core if k == 0 else 1 - core
        for r in range(k ^ 1, chips):
            send(row_p, gather_p.at[slot], 9, chip_at(lax.rem(chip + r, chips), kk))

    settle(ring_in_us.at[pl.ds(0, walks - 1)], 8)
    row = ring_in_us[0]
    for v in range(1, walks):
        row = row + ring_in_us[v]
    row_us[...] = row
    gather_us[slot] = row
    for k in range(2):
        kk = core if k == 0 else 1 - core
        for r in range(k ^ 1, chips):
            send(row_us, gather_us.at[slot], 10, chip_at(lax.rem(chip + r, chips), kk))

    settle(gring_in.at[pl.ds(0, walks - 1)], 7)
    gsum = gring_in[0]
    for v in range(1, walks):
        gsum = gsum + gring_in[v]
    geo_out_ref[...] = gsum

    settle(gather_p.at[pl.ds(0, 2 * chips - 1)], 9)
    for k in range(2):
        part = gather_p[k * chips].astype(F32)
        for c in range(1, chips):
            part = part + gather_p[k * chips + c].astype(F32)
        share_ref[1, :, pl.ds(k * lanes, lanes)] = part
    settle(gather_us.at[pl.ds(0, 2 * chips - 1)], 10)
    for n in range(2):
        for k in range(2):
            for c in range(chips):
                share_ref[2 * n, pl.ds(c, 1), pl.ds(k * lanes, lanes)] = gather_us[k * chips + c, pl.ds(n, 1), :]


def last_kernel(newf, df, share, geo, newf_out, df_out, gs_out, gp_out, gu_out, geo_out, sem):
    copies = [
        pltpu.make_async_copy(src, dst, sem.at[n])
        for n, (src, dst) in enumerate((
            (df, df_out), (newf, newf_out), (share.at[0], gs_out), (share.at[1], gp_out), (share.at[2], gu_out), (geo, geo_out),
        ))
    ]
    for c in copies:
        c.start()
    for c in copies:
        c.wait()


def vmem(n):
    return [pl.BlockSpec(memory_space=pltpu.VMEM)] * n


def hbm(n):
    return [pl.BlockSpec(memory_space=pltpu.HBM)] * n


def body(sizes, features, w_self, w_pair, w_update, geo_embed, lattice, neighbours, counts, envelope, cotangent):
    slabs, walks, geoms = sizes
    feats, cot = features[0], cotangent[0]
    walkers, rows, width = feats.shape
    slots = neighbours.shape[3]
    lats = geo_embed.shape[1]
    wide = 2 * rows
    nbr = jnp.swapaxes(neighbours[0], 1, 2)
    env = jnp.swapaxes(envelope[0], 1, 2)
    sds = jax.ShapeDtypeStruct
    scr = pltpu.VMEM
    dma = pltpu.SemaphoreType.DMA
    smem = [pl.BlockSpec(memory_space=pltpu.SMEM)]
    rim = sds((walkers, RIM, width), BF16)
    before, after, weights, p, turn, slide, feats_v = pl.pallas_call(
        functools.partial(first_kernel, slabs),
        out_shape=(
            rim,
            rim,
            sds((walkers, slots, rows), F32),
            sds((walkers * width, STEPS * rows), F32),
            sds((rows, STEPS * rows), BF16),
            sds((wide, len(BASES) * wide), BF16),
            sds((walkers, rows, width), BF16),
        ),
        in_specs=smem + hbm(6),
        out_specs=vmem(7),
        scratch_shapes=[
            scr((walkers, slots, rows), jnp.int32),
            scr((walkers, slots, rows), BF16),
            scr((walkers, rows), jnp.int32),
            scr((width, width), BF16),
            scr((lats, width), F32),
            scr((slots, rows), jnp.int32),
            scr((slots, rows), F32),
            dma((6,)),
            dma((2,)),
            dma((2,)),
        ],
        compiler_params=pltpu.CompilerParams(collective_id=0, has_side_effects=True, vmem_limit_bytes=12 * MIB),
        name="first",
    )(lattice, feats, nbr, env, counts[0], w_self, geo_embed[0])

    chips = slabs * geoms // 2
    lanes = width // 2
    share_rows = width // walks
    newf, df, share, geo = pl.pallas_call(
        functools.partial(main_kernel, slabs, walks, geoms),
        out_shape=(
            sds((walkers, rows, width), BF16),
            sds((walkers, rows, width), F32),
            sds((3, share_rows, width), F32),
            sds((lats, width), F32),
        ),
        in_specs=smem + vmem(8) + hbm(4),
        out_specs=vmem(4),
        scratch_shapes=[
            scr((width, width), BF16),
            scr((width, width), BF16),
            scr((width, width), BF16),
            scr((walkers, rows, width), BF16),
            scr((walkers, wide, width), BF16),
            scr((walkers, width, wide), BF16),
            scr((walkers * width, len(BASES) * wide), F32),
            scr((slots, walkers * width, rows), F32),
            scr((walkers * width, STEPS * rows), BF16),
            scr((walkers * width, STEPS * rows), BF16),
            scr((walkers * width, STEPS * rows), F32),
            scr((walkers * width, len(BASES) * wide), BF16),
            scr((walkers, rows, width), F32),
            scr((2, walkers, RIM, width), BF16),
            scr((2, walkers, RIM, width), BF16),
            scr((3, width, width), F32),
            scr((2, width, lanes), F32),
            scr((width, lanes), BF16),
            scr((2, width, lanes), BF16),
            scr((2, width, lanes), BF16),
            scr((width, lanes), BF16),
            scr((width, lanes), BF16),
            scr((chips, 2, walks, lanes), BF16),
            scr((chips, 2, walks, lanes), BF16),
            scr((walks, 2, lanes), F32),
            scr((walks, 2, lanes), F32),
            scr((walks, share_rows, lanes), BF16),
            scr((walks, share_rows, lanes), BF16),
            scr((2, lanes), F32),
            scr((2 * chips, 2, lanes), F32),
            scr((share_rows, lanes), BF16),
            scr((2 * chips, share_rows, lanes), BF16),
            scr((lats, width), F32),
            scr((slabs, lats, width), F32),
            scr((lats, width), F32),
            scr((walks, lats, width), F32),
            dma((4,)),
            dma((11,)),
            dma((11,)),
        ],
        compiler_params=pltpu.CompilerParams(collective_id=1, has_side_effects=True, vmem_limit_bytes=44 * MIB),
        name="main",
    )(lattice, counts[0], before, after, weights, p, turn, slide, feats_v, w_self, w_pair, w_update, cot)

    block = sds((share_rows, width), F32)
    newf, df, gs, gp, gu, geo = pl.pallas_call(
        last_kernel,
        out_shape=(
            sds((walkers, rows, width), BF16),
            sds((walkers, rows, width), F32),
            block,
            block,
            block,
            sds((lats, width), F32),
        ),
        in_specs=vmem(4),
        out_specs=hbm(6),
        scratch_shapes=[dma((6,))],
        compiler_params=pltpu.CompilerParams(vmem_limit_bytes=4 * MIB),
        name="last",
    )(newf, df, share, geo)
    return newf[None], df[None], gs, gp, gu, geo[None]


def solution(mesh):
    sizes = (mesh.shape["slab"], mesh.shape["walker"], mesh.shape["geom"])
    return jax.shard_map(
        functools.partial(body, sizes),
        mesh=mesh,
        in_specs=(
            P("geom", "walker", "slab", None),
            P(),
            P(),
            P(),
            P("geom", None, None),
            P("geom", "walker"),
            P("geom", "walker", "slab", None),
            P("geom", "walker", "slab"),
            P("geom", "walker", "slab", None),
            P("geom", "walker", "slab", None),
        ),
        out_specs=(
            P("geom", "walker", "slab", None),
            P("geom", "walker", "slab", None),
            P("walker", None),
            P("walker", None),
            P("walker", None),
            P("geom", None, None),
        ),
        check_vma=False,
    )
```

time: 570 us -> 68.2 us (0.12)
  blocking collectives: 489 us -> 0 us
  Pallas kernels: 0 us -> 56.8 us
  matrix products: 28.9 us -> 0 us
  starting transfers between devices: 18.8 us -> 0 us
  between operations: 14 us -> 0.68 us
  other arithmetic: 10.5 us -> 0 us
    psum x2 -> x0, blocking collectives: 489 us -> none  [the longest x1 310 us: body(): geo_total = lax.psum(geo_local, ('slab', 'walker'))]
    pallas_call x0 -> x3, Pallas kernels: none -> 56.8 us  [the longest x1 46.7 us: body(): pl.pallas_call(functools.partial(main_kernel, slabs, walks, geoms), out_s...]
    dot_general x17 -> x0, matrix products: 28.9 us -> none  [the longest x2 11.9 us: walker_work(): jnp.einsum('bksm,bksf->bmf', onehot.astype(jnp.float32), d_pre.reshape(bl...]
    ppermute x4 -> x0, starting transfers between devices: 18.7 us -> none  [the longest x2 8.9 us: shifted(): return lax.ppermute(block, axis, route)]
    reduce_sum x3 -> x0, other arithmetic: 8.24 us -> none  [the longest x2 8.2 us: walker_work(): d_self = jnp.sum(d_pre, axis=1)]
  transfers between devices with their start and end apart: 7 -> 0, of which waited for: 0 -> 0; matrix products, arithmetic and copies ran while one was open for 2% -> 0% of each run, Pallas kernels for 0% -> 0%
where the time goes in v2:
time: 68.2 us; the launch traced here: 67.8 us
  Pallas kernels  56.8 us (83%)
  local copies, waits for them, and re-layouts  10.4 us (15%)
    pallas_call x1, Pallas kernels, body(): pl.pallas_call(functools.partial(main_kernel, slabs, walks, geoms), out_s...  46.7 us
    unnamed x26, local copies, waits for them, and re-layouts  10.4 us
    pallas_call x1, Pallas kernels, body(): pl.pallas_call(functools.partial(first_kernel, slabs), out_shape=(rim, ri...  9.28 us

profile of v2, /device:TPU:1, one launch (start us, length us, event | category | flops | bytes accessed | tf_op | source)
XLA Modules:
  0.0 67.8 jit_solution(8725207412091118994)
XLA Ops:
  0.6 0.0 copy-start
  0.6 0.9 %copy-done = bf16[256,256]{1,0:T(8,128)(2,1)S(1)} copy-done((bf16[256,256]{1,0:T(8,128)(2,1)S(1)}, bf16[256,256]{1,0:T(8,128)(2,1)}, u32[]{:S(2)}) %copy-start) | copy-done | bytes 131096
  1.5 0.0 copy-start.5
  1.5 0.9 %copy-done.5 = bf16[1,2,128,256]{3,2,1,0:T(8,128)(2,1)S(1)} copy-done((bf16[1,2,128,256]{3,2,1,0:T(8,128)(2,1)S(1)}, bf16[1,2,128,256]{3,2,1,0:T(8,128)(2,1)}, u32[]{:S(2)}) %copy-start.5) | copy-done | bytes 131096
  2.4 0.0 copy-start.6
  2.4 0.8 %copy-done.6 = s32[1,2,128,64]{2,3,1,0:T(8,128)S(1)} copy-done((s32[1,2,128,64]{2,3,1,0:T(8,128)S(1)}, s32[1,2,128,64]{2,3,1,0:T(8,128)}, u32[]{:S(2)}) %copy-start.6) | copy-done | bytes 65560
  3.3 0.0 copy-start.7
  3.3 0.8 %copy-done.7 = bf16[1,2,128,64]{2,3,1,0:T(8,128)(2,1)S(1)} copy-done((bf16[1,2,128,64]{2,3,1,0:T(8,128)(2,1)S(1)}, bf16[1,2,128,64]{2,3,1,0:T(8,128)(2,1)}, u32[]{:S(2)}) %copy-start.7) | copy-done | bytes 32792
  4.0 0.0 copy-start.8
  4.0 0.7 copy-done.8
  4.7 0.0 copy-start.10
  4.7 0.7 %copy-done.10 = f32[1,2,256]{2,1,0:T(2,128)S(1)} copy-done((f32[1,2,256]{2,1,0:T(2,128)S(1)}, f32[1,2,256]{2,1,0:T(2,128)}, u32[]{:S(2)}) %copy-start.10) | copy-done | bytes 2072
  5.4 0.0 copy-start.11
  5.4 0.7 copy-done.11
  6.1 9.3 %first.1 = (bf16[2,32,256]{2,1,0:T(8,128)(2,1)S(1)}, bf16[2,32,256]{2,1,0:T(8,128)(2,1)S(1)}, f32[2,64,128]{2,1,0:T(8,128)S(1)}, f32[512,1024]{1,0:T(8,128)S(1)}...) custom-call(s32[1,2]{1,0:T(1,128)S(1)} %copy-done.11, ...), custom_call_target="tpu_custom_call" | custom-call | tf_op jit(solution)/shard_map/first/pallas_call | solution.py:412
  15.3 0.0 copy-start.1
  15.4 0.9 %copy-done.1 = bf16[256,256]{1,0:T(8,128)(2,1)S(1)} copy-done((bf16[256,256]{1,0:T(8,128)(2,1)S(1)}, bf16[256,256]{1,0:T(8,128)(2,1)}, u32[]{:S(2)}) %copy-start.1) | copy-done | bytes 131096
  16.3 0.0 copy-start.2
  16.3 0.9 %copy-done.2 = bf16[256,256]{1,0:T(8,128)(2,1)S(1)} copy-done((bf16[256,256]{1,0:T(8,128)(2,1)S(1)}, bf16[256,256]{1,0:T(8,128)(2,1)}, u32[]{:S(2)}) %copy-start.2) | copy-done | bytes 131096
  17.2 0.0 copy-start.3
  17.2 0.9 %copy-done.3 = bf16[256,256]{1,0:T(8,128)(2,1)S(1)} copy-done((bf16[256,256]{1,0:T(8,128)(2,1)S(1)}, bf16[256,256]{1,0:T(8,128)(2,1)}, u32[]{:S(2)}) %copy-start.3) | copy-done | bytes 131096
  18.1 0.0 copy-start.4
  18.1 0.9 %copy-done.4 = bf16[1,2,128,256]{3,2,1,0:T(8,128)(2,1)S(1)} copy-done((bf16[1,2,128,256]{3,2,1,0:T(8,128)(2,1)S(1)}, bf16[1,2,128,256]{3,2,1,0:T(8,128)(2,1)}, u32[]{:S(2)}) %copy-start.4) | copy-done | bytes 131096
  19.0 0.0 copy-start.9
  19.0 0.7 copy-done.9
  19.7 0.0 copy-start.12
  19.7 0.7 copy-done.12
  20.3 46.7 %main.1 = (bf16[2,128,256]{2,1,0:T(8,128)(2,1)S(1)}, f32[2,128,256]{2,1,0:T(8,128)S(1)}, f32[3,16,256]{2,1,0:T(8,128)S(1)}, f32[2,256]{1,0:T(2,128)S(1)}) custom-call(s32[1,2]{1,0:T(1,128)S(1)} %copy-done.12, s32[2,128]{1,0:T(2,128)S(1)} %bitcast.18, bf16[2,32,256]{2,1,0:T(8,128)(2,1)S(1)} %get-tuple-element.23.before_ref, ...), custom_call_target="tpu_custom_call" | custom-call | tf_op jit(solution)/shard_map/main/pallas_call | solution.py:444
  67.0 0.8 %last.1 = (bf16[2,128,256]{2,1,0:T(8,128)(2,1)}, f32[2,128,256]{2,1,0:T(8,128)}, f32[16,256]{1,0:T(8,128)}, f32[16,256]{1,0:T(8,128)}, f32[16,256]{1,0:T(8,128)}, /*index=5*/f32[2,256]{1,0:T(2,128)}) custom-call(bf16[2,128,256]{2,1,0:T(8,128)(2,1)S(1)} %get-tuple-element.30.newf, f32[2,128,256]{2,1,0:T(8,128)S(1)} %get-tuple-element.31.df, ...), custom_call_target="tpu_custom_call" | custom-call | tf_op jit(solution)/shard_map/last/pallas_call | solution.py:500
Async XLA Ops:
  0.6 0.9 %copy-start = (bf16[256,256]{1,0:T(8,128)(2,1)S(1)}, bf16[256,256]{1,0:T(8,128)(2,1)}, u32[]{:S(2)}) copy-start(bf16[256,256]{1,0:T(8,128)(2,1)} %ws_hbm.3) | copy-start | bytes 393220
  1.5 0.9 %copy-start.5 = (bf16[1,2,128,256]{3,2,1,0:T(8,128)(2,1)S(1)}, bf16[1,2,128,256]{3,2,1,0:T(8,128)(2,1)}, u32[]{:S(2)}) copy-start(bf16[1,2,128,256]{3,2,1,0:T(8,128)(2,1)} %param.10) | copy-start | bytes 393220
  2.4 0.8 %copy-start.6 = (s32[1,2,128,64]{2,3,1,0:T(8,128)S(1)}, s32[1,2,128,64]{2,3,1,0:T(8,128)}, u32[]{:S(2)}) copy-start(s32[1,2,128,64]{2,3,1,0:T(8,128)} %param.16) | copy-start | bytes 196612
  3.3 0.8 %copy-start.7 = (bf16[1,2,128,64]{2,3,1,0:T(8,128)(2,1)S(1)}, bf16[1,2,128,64]{2,3,1,0:T(8,128)(2,1)}, u32[]{:S(2)}) copy-start(bf16[1,2,128,64]{2,3,1,0:T(8,128)(2,1)} %param.18) | copy-start | bytes 98308
  4.0 0.7 %copy-start.8 = (s32[1,2,128]{2,1,0:T(2,128)S(1)}, s32[1,2,128]{2,1,0:T(2,128)}, u32[]{:S(2)}) copy-start(s32[1,2,128]{2,1,0:T(2,128)} %param.17) | copy-start | bytes 3076
  4.7 0.7 %copy-start.10 = (f32[1,2,256]{2,1,0:T(2,128)S(1)}, f32[1,2,256]{2,1,0:T(2,128)}, u32[]{:S(2)}) copy-start(f32[1,2,256]{2,1,0:T(2,128)} %param.14) | copy-start | bytes 6148
  5.4 0.7 copy-start.11
  15.3 0.9 %copy-start.1 = (bf16[256,256]{1,0:T(8,128)(2,1)S(1)}, bf16[256,256]{1,0:T(8,128)(2,1)}, u32[]{:S(2)}) copy-start(bf16[256,256]{1,0:T(8,128)(2,1)} %ws_hbm.3) | copy-start | bytes 393220
  16.3 0.9 %copy-start.2 = (bf16[256,256]{1,0:T(8,128)(2,1)S(1)}, bf16[256,256]{1,0:T(8,128)(2,1)}, u32[]{:S(2)}) copy-start(bf16[256,256]{1,0:T(8,128)(2,1)} %wp_hbm.1) | copy-start | bytes 393220
  17.2 0.9 %copy-start.3 = (bf16[256,256]{1,0:T(8,128)(2,1)S(1)}, bf16[256,256]{1,0:T(8,128)(2,1)}, u32[]{:S(2)}) copy-start(bf16[256,256]{1,0:T(8,128)(2,1)} %wu_hbm.1) | copy-start | bytes 393220
  18.1 0.9 %copy-start.4 = (bf16[1,2,128,256]{3,2,1,0:T(8,128)(2,1)S(1)}, bf16[1,2,128,256]{3,2,1,0:T(8,128)(2,1)}, u32[]{:S(2)}) copy-start(bf16[1,2,128,256]{3,2,1,0:T(8,128)(2,1)} %param.19) | copy-start | bytes 393220
  19.0 0.7 %copy-start.9 = (s32[1,2,128]{2,1,0:T(2,128)S(1)}, s32[1,2,128]{2,1,0:T(2,128)}, u32[]{:S(2)}) copy-start(s32[1,2,128]{2,1,0:T(2,128)} %param.17) | copy-start | bytes 3076
  19.7 0.7 copy-start.12

commit v3 on v2

--- a/solution.py
+++ b/solution.py
@@ -87,11 +87,11 @@
                     h = jnp.where(lane < a, q_ref[here, (2 * b + 1) * rows : (2 * b + 2) * rows], h)
                 h = h + pa
                 u = 1.0 + jnp.tanh(h)
-                g = h * u
-                wm = w_ref[w, pl.ds(m, 1), :]
-                t = wm * (u + g * (2.0 - u))
+                wu = u * w_ref[w, pl.ds(m, 1), :]
+                wg = h * wu
+                t = wu + wg * (2.0 - u)
                 t_ref[m, here, :] = t
-                ga.append(wm * g)
+                ga.append(wg)
                 sa.append(t)
             while len(ga) > 1:
                 ga = [ga[n] + ga[n + 1] for n in range(0, len(ga), 2)]
@@ -127,9 +127,9 @@
 
 
 def first_kernel(
-    slabs, lat_ref, feats_hbm, nbr_hbm, env_hbm, cnt_hbm, ws_hbm, geo_hbm,
-    before_ref, after_ref, w_ref, p_ref, turn_ref, slide_ref, feats_ref,
-    nbr_ref, env_ref, cnt_ref, ws_ref, geo_ref, off_ref, wt_ref, load_sem, send_sem, recv_sem,
+    slabs, lat_hbm, feats_hbm, nbr_hbm, env_hbm, cnt_hbm, ws_hbm, geo_hbm,
+    before_ref, after_ref, w_ref, p_ref, turn_ref, slide_ref, feats_ref, inv_ref, member_ref,
+    lat_ref, nbr_ref, env_ref, cnt_ref, ws_ref, geo_ref, off_ref, wt_ref, load_sem, send_sem, recv_sem,
 ):
     me = lax.axis_index("slab")
     nxt, prv = lax.rem(me + 1, slabs), lax.rem(me + slabs - 1, slabs)
@@ -138,7 +138,7 @@
     pl.semaphore_signal(barrier, inc=1, **at(slab=prv))
     loads = []
     for n, (src, dst) in enumerate((
-        (feats_hbm, feats_ref), (nbr_hbm, nbr_ref), (env_hbm, env_ref), (cnt_hbm, cnt_ref), (ws_hbm, ws_ref), (geo_hbm, geo_ref),
+        (feats_hbm, feats_ref), (nbr_hbm, nbr_ref), (env_hbm, env_ref), (cnt_hbm, cnt_ref), (ws_hbm, ws_ref), (geo_hbm, geo_ref), (lat_hbm, lat_ref),
     )):
         loads.append(pltpu.make_async_copy(src, dst, load_sem.at[n]))
         loads[-1].start()
@@ -157,10 +157,13 @@
     down.start()
     ws_t = ws_ref[...].T
     geo = geo_ref[...]
+    inv_ref[...] = 1.0 / cnt_ref[...].astype(F32)
     for w in range(walkers):
         w_ref[w] = slot_weights(nbr_ref[w], env_ref[w], cnt_ref[pl.ds(w, 1), :], off_ref, wt_ref)
         lats = geo.shape[0]
-        row = jnp.sum(jnp.where(iota((lats, width), 0) == lat_ref[0, w], geo, 0.0), axis=0, keepdims=True)
+        member = (iota((lats, width), 0) == lat_ref[0, w]).astype(F32)
+        member_ref[w] = member
+        row = jnp.sum(jnp.where(member > 0.0, geo, 0.0), axis=0, keepdims=True)
         p = (dot(feats_ref[w], ws_ref[...], NN) + row).T
         p_ref[w * width : (w + 1) * width, :] = split_dot(0.5 * p, turn_ref[...], NN)
     up.wait()
@@ -169,11 +172,11 @@
 
 def main_kernel(
     slabs, walks, geoms,
-    lat_ref, cnt_ref, before_ref, after_ref, w_ref, p_ref, turn_ref, slide_ref, feats_ref, ws_hbm, wp_hbm, wu_hbm, cot_hbm,
+    before_ref, after_ref, w_ref, p_ref, turn_ref, slide_ref, feats_ref, inv_ref, member_ref, ws_hbm, wp_hbm, wu_hbm, cot_hbm,
     newf_ref, df_ref, share_ref, geo_out_ref,
     ws_ref, wp_ref, wu_ref, cot_ref, ext_ref, ext_t_ref, q_ref, t_ref, agg_ref, tot_ref, d_ref, v_ref, own_ref,
     rim_out, rim_in, grads_ref, half_us, half_p,
-    core_out_us, core_in_us, core_out_p, core_in_p, plane_out, plane_in, ring_out_us, ring_in_us, ring_out_p, ring_in_p,
+    core_in_us, core_in_p, plane_out, plane_in, ring_out_us, ring_in_us, ring_out_p, ring_in_p,
     row_us, gather_us, row_p, gather_p, gslab_out, gslab_in, gring_out, gring_in,
     load_sem, send_sem, recv_sem,
 ):
@@ -234,7 +237,7 @@
     dps = []
     for w in range(walkers):
         part = slice(w * width, (w + 1) * width)
-        inv = 1.0 / cnt_ref[pl.ds(w, 1), :].astype(F32)
+        inv = inv_ref[pl.ds(w, 1), :]
         agg_t = (dot(agg_ref[part, :], turn_ref[...], NT) * inv).astype(BF16)
         upd = dot(agg_t.T, wu_ref[...], NN)
         sig = 0.5 + 0.5 * jnp.tanh(0.5 * upd)
@@ -243,8 +246,7 @@
         dd = 0.5 * dot(wu_ref[...], du, NT) * inv
         d_ref[part, :] = split_dot(dd, turn_ref[...], NN)
         dp = (dd * dot(tot_ref[part, :], turn_ref[...], NT)).T
-        mine = iota((lats, width), 0) == lat_ref[0, w]
-        dgeo = dgeo + jnp.where(mine, jnp.sum(dp, axis=0, keepdims=True), 0.0)
+        dgeo = dgeo + jnp.where(member_ref[w] > 0.0, jnp.sum(dp, axis=0, keepdims=True), 0.0)
         dp = dp.astype(BF16)
         dps.append(dp)
         feats_t = feats_ref[w].T
@@ -256,9 +258,8 @@
 
     mine = pl.ds(pl.multiple_of(core * lanes, lanes), lanes)
     theirs = pl.ds(pl.multiple_of((1 - core) * lanes, lanes), lanes)
-    core_out_us[...] = grads_ref[pl.ds(0, 2), :, theirs].astype(BF16)
     pl.semaphore_wait(barrier, 2 * chips - 1 + walks - 1)
-    cross = send(core_out_us, core_in_us, 0, at(geom=pair + 1 - core))
+    cross = send(grads_ref.at[pl.ds(0, 2), :, theirs], core_in_us, 0, at(geom=pair + 1 - core))
     gslab_in[slab] = gslab_out[...]
     for r in range(1, slabs):
         send(gslab_out, gslab_in.at[slab], 1, at(slab=lax.rem(slab + r, slabs)))
@@ -266,7 +267,7 @@
     backward_pass(0, tiles // 2, d_ref, t_ref, v_ref)
 
     cross.wait()
-    half_us[...] = grads_ref[pl.ds(0, 2), :, mine] + core_in_us[...].astype(F32)
+    half_us[...] = grads_ref[pl.ds(0, 2), :, mine] + core_in_us[...]
     for c in range(chips):
         for n in range(2):
             plane_out[c, n] = half_us[n, pl.ds(c, walks, stride=chips), :].astype(BF16)
@@ -276,27 +277,6 @@
         send(plane_out.at[to], plane_in.at[chip], 2, chip_at(to, core))
 
     backward_pass(tiles // 2, tiles // 2, d_ref, t_ref, v_ref)
-
-    for w in range(walkers):
-        dq = dot(v_ref[w * width : (w + 1) * width, :], slide_ref[...], NT).T
-        own_ref[w] = dq[RIM : RIM + rows]
-        dqb = dq.astype(BF16)
-        rim_out[0, w] = dqb[:RIM]
-        rim_out[1, w] = dqb[RIM + rows : 2 * RIM + rows]
-        term = dot(ext_t_ref[w], dqb, NN)
-        grads_ref[2] = term if w == 0 else grads_ref[2] + term
-    core_out_p[...] = grads_ref[2, :, theirs].astype(BF16)
-    cross = send(core_out_p, core_in_p, 3, at(geom=pair + 1 - core))
-    down = send(rim_out.at[0], rim_in.at[0], 4, at(slab=prv))
-    up = send(rim_out.at[1], rim_in.at[1], 5, at(slab=nxt))
-    cross.wait()
-    half_p[...] = (grads_ref[2, :, mine] + core_in_p[...].astype(F32)).astype(BF16)
-    for v in range(walks):
-        ring_out_p[v] = half_p[pl.ds(v * (width // walks), width // walks), :]
-    ring_in_p[z] = ring_out_p[z]
-    for r in range(1, walks):
-        to = lax.rem(z + r, walks)
-        send(ring_out_p.at[to], ring_in_p.at[z], 6, at(walker=to))
 
     settle(gslab_in.at[pl.ds(0, slabs - 1)], 1)
     gsum = gslab_in[0]
@@ -306,6 +286,26 @@
     gring_in[z] = gsum
     for r in range(1, walks):
         send(gring_out, gring_in.at[z], 7, at(walker=lax.rem(z + r, walks)))
+
+    for w in range(walkers):
+        dq = dot(v_ref[w * width : (w + 1) * width, :], slide_ref[...], NT).T
+        own_ref[w] = dq[RIM : RIM + rows]
+        dqb = dq.astype(BF16)
+        rim_out[0, w] = dqb[:RIM]
+        rim_out[1, w] = dqb[RIM + rows : 2 * RIM + rows]
+        term = dot(ext_t_ref[w], dqb, NN)
+        grads_ref[2] = term if w == 0 else grads_ref[2] + term
+    cross = send(grads_ref.at[2, :, theirs], core_in_p, 3, at(geom=pair + 1 - core))
+    down = send(rim_out.at[0], rim_in.at[0], 4, at(slab=prv))
+    up = send(rim_out.at[1], rim_in.at[1], 5, at(slab=nxt))
+    cross.wait()
+    half_p[...] = (grads_ref[2, :, mine] + core_in_p[...]).astype(BF16)
+    for v in range(walks):
+        ring_out_p[v] = half_p[pl.ds(v * (width // walks), width // walks), :]
+    ring_in_p[z] = ring_out_p[z]
+    for r in range(1, walks):
+        to = lax.rem(z + r, walks)
+        send(ring_out_p.at[to], ring_in_p.at[z], 6, at(walker=to))
 
     settle(plane_in.at[pl.ds(0, chips - 1)], 2)
     part = plane_in[0].astype(F32)
@@ -393,6 +393,10 @@
 
 def hbm(n):
     return [pl.BlockSpec(memory_space=pltpu.HBM)] * n
+
+
+def far(*arrays):
+    return [pltpu.with_memory_space_constraint(x, pltpu.HBM) for x in arrays]
 
 
 def body(sizes, features, w_self, w_pair, w_update, geo_embed, lattice, neighbours, counts, envelope, cotangent):
@@ -407,9 +411,8 @@
     sds = jax.ShapeDtypeStruct
     scr = pltpu.VMEM
     dma = pltpu.SemaphoreType.DMA
-    smem = [pl.BlockSpec(memory_space=pltpu.SMEM)]
     rim = sds((walkers, RIM, width), BF16)
-    before, after, weights, p, turn, slide, feats_v = pl.pallas_call(
+    before, after, weights, p, turn, slide, feats_v, inv, member = pl.pallas_call(
         functools.partial(first_kernel, slabs),
         out_shape=(
             rim,
@@ -419,10 +422,13 @@
             sds((rows, STEPS * rows), BF16),
             sds((wide, len(BASES) * wide), BF16),
             sds((walkers, rows, width), BF16),
+            sds((walkers, rows), F32),
+            sds((walkers, lats, width), F32),
         ),
-        in_specs=smem + hbm(6),
-        out_specs=vmem(7),
+        in_specs=hbm(7),
+        out_specs=vmem(9),
         scratch_shapes=[
+            pltpu.SMEM((1, walkers), jnp.int32),
             scr((walkers, slots, rows), jnp.int32),
             scr((walkers, slots, rows), BF16),
             scr((walkers, rows), jnp.int32),
@@ -430,13 +436,13 @@
             scr((lats, width), F32),
             scr((slots, rows), jnp.int32),
             scr((slots, rows), F32),
-            dma((6,)),
+            dma((7,)),
             dma((2,)),
             dma((2,)),
         ],
         compiler_params=pltpu.CompilerParams(collective_id=0, has_side_effects=True, vmem_limit_bytes=12 * MIB),
         name="first",
-    )(lattice, feats, nbr, env, counts[0], w_self, geo_embed[0])
+    )(*far(lattice, feats, nbr, env, counts[0], w_self, geo_embed[0]))
 
     chips = slabs * geoms // 2
     lanes = width // 2
@@ -449,7 +455,7 @@
             sds((3, share_rows, width), F32),
             sds((lats, width), F32),
         ),
-        in_specs=smem + vmem(8) + hbm(4),
+        in_specs=vmem(9) + hbm(4),
         out_specs=vmem(4),
         scratch_shapes=[
             scr((width, width), BF16),
@@ -470,10 +476,8 @@
             scr((3, width, width), F32),
             scr((2, width, lanes), F32),
             scr((width, lanes), BF16),
-            scr((2, width, lanes), BF16),
-            scr((2, width, lanes), BF16),
-            scr((width, lanes), BF16),
-            scr((width, lanes), BF16),
+            scr((2, width, lanes), F32),
+            scr((width, lanes), F32),
             scr((chips, 2, walks, lanes), BF16),
             scr((chips, 2, walks, lanes), BF16),
             scr((walks, 2, lanes), F32),
@@ -494,7 +498,7 @@
         ],
         compiler_params=pltpu.CompilerParams(collective_id=1, has_side_effects=True, vmem_limit_bytes=44 * MIB),
         name="main",
-    )(lattice, counts[0], before, after, weights, p, turn, slide, feats_v, w_self, w_pair, w_update, cot)
+    )(before, after, weights, p, turn, slide, feats_v, inv, member, *far(w_self, w_pair, w_update, cot))
 
     block = sds((share_rows, width), F32)
     newf, df, gs, gp, gu, geo = pl.pallas_call(

time: 68.2 us -> 56.5 us (0.83)
  local copies, waits for them, and re-layouts: 10.4 us -> 0 us
  Pallas kernels: 56.8 us -> 55.7 us
    unnamed x26 -> x0, local copies, waits for them, and re-layouts: 10.4 us -> none
    pallas_call x1, Pallas kernels: 46.7 us -> 45.8 us  [body(): pl.pallas_call(functools.partial(main_kernel, slabs, walks, geoms), out_s...]
where the time goes in v3:
time: 56.5 us; the launch traced here: 56.4 us
  Pallas kernels  55.7 us (99%)
  between operations  0.65 us (1%)
    pallas_call x1, Pallas kernels, body(): pl.pallas_call(functools.partial(main_kernel, slabs, walks, geoms), out_s...  45.8 us
    pallas_call x1, Pallas kernels, body(): pl.pallas_call(functools.partial(first_kernel, slabs), out_shape=(rim, ri...  9.12 us

profile of v3, /device:TPU:1, one launch (start us, length us, event | category | flops | bytes accessed | tf_op | source)
XLA Modules:
  0.0 56.4 jit_solution(6956746313440198889)
XLA Ops:
  0.6 9.1 %first.1 = (bf16[2,32,256]{2,1,0:T(8,128)(2,1)S(1)}, bf16[2,32,256]{2,1,0:T(8,128)(2,1)S(1)}, f32[2,64,128]{2,1,0:T(8,128)S(1)}, f32[512,1024]{1,0:T(8,128)S(1)}...) custom-call(s32[1,2]{1,0:T(1,128)} %lat_hbm.1, ...), custom_call_target="tpu_custom_call" | custom-call | tf_op jit(solution)/shard_map/first/pallas_call | solution.py:415
  9.8 45.8 %main.1 = (bf16[2,128,256]{2,1,0:T(8,128)(2,1)S(1)}, f32[2,128,256]{2,1,0:T(8,128)S(1)}, f32[3,16,256]{2,1,0:T(8,128)S(1)}, f32[2,256]{1,0:T(2,128)S(1)}) custom-call(bf16[2,32,256]{2,1,0:T(8,128)(2,1)S(1)} %get-tuple-element.25.before_ref, bf16[2,32,256]{2,1,0:T(8,128)(2,1)S(1)} %get-tuple-element.26.after_ref, f32[2,64,128]{2,1,0:T(8,128)S(1)} %get-tuple-element.27.w_ref, ...), custom_call_target="tpu_custom_call" | custom-call | tf_op jit(solution)/shard_map/main/pallas_call | solution.py:450
  55.5 0.8 %last.1 = (bf16[2,128,256]{2,1,0:T(8,128)(2,1)}, f32[2,128,256]{2,1,0:T(8,128)}, f32[16,256]{1,0:T(8,128)}, f32[16,256]{1,0:T(8,128)}, f32[16,256]{1,0:T(8,128)}, /*index=5*/f32[2,256]{1,0:T(2,128)}) custom-call(bf16[2,128,256]{2,1,0:T(8,128)(2,1)S(1)} %get-tuple-element.34.newf, f32[2,128,256]{2,1,0:T(8,128)S(1)} %get-tuple-element.35.df, ...), custom_call_target="tpu_custom_call" | custom-call | tf_op jit(solution)/shard_map/last/pallas_call | solution.py:504

commit v4 on v3

--- a/solution.py
+++ b/solution.py
@@ -11,9 +11,10 @@
 F32 = jnp.float32
 BF16 = jnp.bfloat16
 MESH = pl.DeviceIdType.MESH
-BASES = (0, 8, 16, 24, 33, 41, 49, 57)
-STEPS = 8
-TILE = 16
+SLOTS = 2 * RIM
+FGROUP = 4
+BGROUP = 8
+TILE = 32
 MIB = 1024 * 1024
 NN = ((1,), (0,))
 NT = ((1,), (1,))
@@ -23,11 +24,6 @@
     return lax.dot_general(a, b, (dims, ((), ())), preferred_element_type=F32)
 
 
-def split_dot(a, b, dims):
-    high = a.astype(BF16)
-    return dot(high, b, dims) + dot((a - high.astype(F32)).astype(BF16), b, dims)
-
-
 def at(**coords):
     return dict(device_id=coords, device_id_type=MESH)
 
@@ -36,15 +32,16 @@
     return lax.broadcasted_iota(jnp.int32, shape, dim)
 
 
-def shift_matrices(turn_ref, slide_ref):
-    rows = turn_ref.shape[0]
-    wide = slide_ref.shape[0]
-    for a in range(STEPS):
-        moved = lax.rem(iota((rows, rows), 0) + a, rows)
-        turn_ref[:, a * rows : (a + 1) * rows] = (moved == iota((rows, rows), 1)).astype(F32).astype(BF16)
-    for b, base in enumerate(BASES):
-        moved = iota((wide, wide), 1) + base
-        slide_ref[:, b * wide : (b + 1) * wide] = (moved == iota((wide, wide), 0)).astype(F32).astype(BF16)
+def window_matrix(slide_ref):
+    wide, rows = slide_ref.shape[0], slide_ref.shape[1] // SLOTS
+    gap = iota((wide, rows), 0) - iota((wide, rows), 1)
+
+    def block(m, carry):
+        off = m + jnp.where(m >= RIM, 1, 0)
+        slide_ref[:, pl.ds(pl.multiple_of(m * rows, rows), rows)] = jnp.where(gap == off, 1.0, 0.0).astype(BF16)
+        return carry
+
+    lax.fori_loop(0, SLOTS, block, 0)
 
 
 def slot_weights(nbr, env, count, off_ref, wt_ref):
@@ -60,75 +57,79 @@
             acc = acc + jnp.where(off_ref[pl.ds(k, 1), :] == slot, wt_ref[pl.ds(k, 1), :], 0.0)
         return acc
 
-    weights = lax.fori_loop(0, slots // 8, place, jnp.zeros((slots, rows), F32))
-    turned = weights
-    sub = lax.rem(slot, STEPS)
-    for a in range(1, STEPS):
-        turned = jnp.where(sub == a, pltpu.roll(weights, a, 1), turned)
-    return turned
-
-
-def forward_pass(walkers, p_ref, q_ref, w_ref, t_ref, agg_ref, tot_ref):
-    rows = w_ref.shape[2]
-    tiles = p_ref.shape[0] // TILE
-    lane = iota((TILE, rows), 1)
-
-    def tile_work(tile, carry):
-        r0 = pl.multiple_of(tile * TILE, TILE)
-        w = tile // (tiles // walkers)
-        here = pl.ds(r0, TILE)
-        for a in range(STEPS):
-            pa = p_ref[here, a * rows : (a + 1) * rows]
-            ga, sa = [], []
-            for b in range(len(BASES)):
-                m = b * STEPS + a
-                h = q_ref[here, 2 * b * rows : (2 * b + 1) * rows]
-                if a:
-                    h = jnp.where(lane < a, q_ref[here, (2 * b + 1) * rows : (2 * b + 2) * rows], h)
-                h = h + pa
+    return lax.fori_loop(0, slots // 8, place, jnp.zeros((slots, rows), F32))
+
+
+def forward_pass(q_ref, p_ref, w_ref, slide_ref, h_ref, t_ref, agg_ref, tot_ref):
+    total, rows = p_ref.shape
+    width = total // w_ref.shape[0]
+    groups = SLOTS // FGROUP
+    agg_ref[...] = jnp.zeros(agg_ref.shape, F32)
+    tot_ref[...] = jnp.zeros(tot_ref.shape, F32)
+
+    def windows(g, at_slot):
+        cols = pl.ds(pl.multiple_of(g * FGROUP * rows, FGROUP * rows), FGROUP * rows)
+        h_ref[at_slot] = dot(q_ref[...], slide_ref[:, cols], NN)
+
+    def work(g, at_slot):
+        for r in range(0, total, TILE):
+            here = slice(r, r + TILE)
+            p = p_ref[here, :]
+            ga = sa = None
+            for x in range(FGROUP):
+                h = h_ref[at_slot, here, x * rows : (x + 1) * rows] + p
                 u = 1.0 + jnp.tanh(h)
-                wu = u * w_ref[w, pl.ds(m, 1), :]
+                wu = u * w_ref[r // width, pl.ds(g * FGROUP + x, 1), :]
                 wg = h * wu
                 t = wu + wg * (2.0 - u)
-                t_ref[m, here, :] = t
-                ga.append(wg)
-                sa.append(t)
-            while len(ga) > 1:
-                ga = [ga[n] + ga[n + 1] for n in range(0, len(ga), 2)]
-                sa = [sa[n] + sa[n + 1] for n in range(0, len(sa), 2)]
-            agg_ref[here, a * rows : (a + 1) * rows] = ga[0].astype(BF16)
-            tot_ref[here, a * rows : (a + 1) * rows] = sa[0].astype(BF16)
+                t_ref[g * FGROUP + x, here, :] = t
+                ga = wg if x == 0 else ga + wg
+                sa = t if x == 0 else sa + t
+            agg_ref[here, :] += ga
+            tot_ref[here, :] += sa
+
+    windows(0, 0)
+
+    def step(i, carry):
+        windows(2 * i + 1, 1)
+        work(2 * i, 0)
+        windows(jnp.minimum(2 * i + 2, groups - 1), 0)
+        work(2 * i + 1, 1)
         return carry
 
-    lax.fori_loop(0, tiles, tile_work, 0)
-
-
-def backward_pass(first, count, d_ref, t_ref, v_ref):
-    rows = t_ref.shape[2]
-    nb = len(BASES)
-    lane = iota((TILE, rows), 1)
-
-    def tile_work(tile, carry):
-        here = pl.ds(pl.multiple_of(tile * TILE, TILE), TILE)
-        ds = [d_ref[here, a * rows : (a + 1) * rows] for a in range(STEPS)]
-        for b in range(nb):
-            total = wrap = None
-            for a in range(STEPS):
-                v = t_ref[b * STEPS + a, here, :] * ds[a]
-                total = v if a == 0 else total + v
-                if a:
-                    c = jnp.where(lane < a, v, 0.0)
-                    wrap = c if a == 1 else wrap + c
-            v_ref[here, 2 * b * rows : (2 * b + 1) * rows] = (total - wrap).astype(BF16)
-            v_ref[here, (2 * b + 1) * rows : (2 * b + 2) * rows] = wrap.astype(BF16)
+    lax.fori_loop(0, groups // 2, step, 0)
+
+
+def backward_pass(first, count, d_ref, t_ref, slide_ref, v_ref, dqt_ref):
+    total, rows = d_ref.shape
+
+    def work(g, at_slot):
+        for r in range(0, total, TILE):
+            here = slice(r, r + TILE)
+            d = d_ref[here, :]
+            for x in range(BGROUP):
+                v_ref[at_slot, here, x * rows : (x + 1) * rows] = (t_ref[g * BGROUP + x, here, :] * d).astype(BF16)
+
+    def gather(g, at_slot):
+        cols = pl.ds(pl.multiple_of(g * BGROUP * rows, BGROUP * rows), BGROUP * rows)
+        dqt_ref[...] += dot(v_ref[at_slot], slide_ref[:, cols], NT)
+
+    work(first, 0)
+
+    def step(i, carry):
+        g = first + 2 * i
+        work(g + 1, 1)
+        gather(g, 0)
+        work(jnp.minimum(g + 2, first + count - 1), 0)
+        gather(g + 1, 1)
         return carry
 
-    lax.fori_loop(first, first + count, tile_work, 0)
+    lax.fori_loop(0, count // 2, step, 0)
 
 
 def first_kernel(
     slabs, lat_hbm, feats_hbm, nbr_hbm, env_hbm, cnt_hbm, ws_hbm, geo_hbm,
-    before_ref, after_ref, w_ref, p_ref, turn_ref, slide_ref, feats_ref, inv_ref, member_ref,
+    before_ref, after_ref, w_ref, p_ref, slide_ref, feats_ref, inv_ref, member_ref,
     lat_ref, nbr_ref, env_ref, cnt_ref, ws_ref, geo_ref, off_ref, wt_ref, load_sem, send_sem, recv_sem,
 ):
     me = lax.axis_index("slab")
@@ -143,7 +144,6 @@
         loads.append(pltpu.make_async_copy(src, dst, load_sem.at[n]))
         loads[-1].start()
     walkers, rows, width = feats_ref.shape
-    shift_matrices(turn_ref, slide_ref)
     for c in loads:
         c.wait()
     pl.semaphore_wait(barrier, 2)
@@ -155,7 +155,7 @@
     )
     up.start()
     down.start()
-    ws_t = ws_ref[...].T
+    window_matrix(slide_ref)
     geo = geo_ref[...]
     inv_ref[...] = 1.0 / cnt_ref[...].astype(F32)
     for w in range(walkers):
@@ -164,17 +164,17 @@
         member = (iota((lats, width), 0) == lat_ref[0, w]).astype(F32)
         member_ref[w] = member
         row = jnp.sum(jnp.where(member > 0.0, geo, 0.0), axis=0, keepdims=True)
-        p = (dot(feats_ref[w], ws_ref[...], NN) + row).T
-        p_ref[w * width : (w + 1) * width, :] = split_dot(0.5 * p, turn_ref[...], NN)
+        p = 0.5 * (dot(feats_ref[w], ws_ref[...], NN) + row)
+        p_ref[w * width : (w + 1) * width, :] = p.T
     up.wait()
     down.wait()
 
 
 def main_kernel(
     slabs, walks, geoms,
-    before_ref, after_ref, w_ref, p_ref, turn_ref, slide_ref, feats_ref, inv_ref, member_ref, ws_hbm, wp_hbm, wu_hbm, cot_hbm,
+    before_ref, after_ref, w_ref, p_ref, slide_ref, feats_ref, inv_ref, member_ref, ws_hbm, wp_hbm, wu_hbm, cot_hbm,
     newf_ref, df_ref, share_ref, geo_out_ref,
-    ws_ref, wp_ref, wu_ref, cot_ref, ext_ref, ext_t_ref, q_ref, t_ref, agg_ref, tot_ref, d_ref, v_ref, own_ref,
+    ws_ref, wp_ref, wu_ref, cot_ref, ext_ref, ext_t_ref, q_ref, h_ref, t_ref, agg_ref, tot_ref, d_ref, v_ref, dqt_ref, upd_ref, dp_ref, own_ref,
     rim_out, rim_in, grads_ref, half_us, half_p,
     core_in_us, core_in_p, plane_out, plane_in, ring_out_us, ring_in_us, ring_out_p, ring_in_p,
     row_us, gather_us, row_p, gather_p, gslab_out, gslab_in, gring_out, gring_in,
@@ -190,7 +190,7 @@
     walkers, rows, width = feats_ref.shape
     lanes = width // 2
     lats = gslab_out.shape[0]
-    tiles = walkers * width // TILE
+    groups = SLOTS // BGROUP
 
     def chip_at(c, k):
         return at(slab=c // half_geoms, geom=lax.rem(c, half_geoms) * 2 + k)
@@ -229,32 +229,30 @@
     for w in range(walkers):
         q = (0.5 * dot(ext_ref[w], wp_ref[...], NN)).astype(BF16)
         ext_t_ref[w] = ext_ref[w].T
-        q_ref[w * width : (w + 1) * width, :] = dot(q.T, slide_ref[...], NN)
-
-    forward_pass(walkers, p_ref, q_ref, w_ref, t_ref, agg_ref, tot_ref)
+        q_ref[w * width : (w + 1) * width, :] = q.T
+
+    forward_pass(q_ref, p_ref, w_ref, slide_ref, h_ref, t_ref, agg_ref, tot_ref)
 
     dgeo = jnp.zeros((lats, width), F32)
-    dps = []
     for w in range(walkers):
         part = slice(w * width, (w + 1) * width)
         inv = inv_ref[pl.ds(w, 1), :]
-        agg_t = (dot(agg_ref[part, :], turn_ref[...], NT) * inv).astype(BF16)
+        agg_t = (agg_ref[part, :] * inv).astype(BF16)
         upd = dot(agg_t.T, wu_ref[...], NN)
         sig = 0.5 + 0.5 * jnp.tanh(0.5 * upd)
-        newf_ref[w] = (feats_ref[w].astype(F32) + upd * sig).astype(BF16)
+        upd_ref[w] = upd * sig
         du = (cot_ref[w].astype(F32) * (sig * (1.0 + upd * (1.0 - sig)))).astype(BF16)
         dd = 0.5 * dot(wu_ref[...], du, NT) * inv
-        d_ref[part, :] = split_dot(dd, turn_ref[...], NN)
-        dp = (dd * dot(tot_ref[part, :], turn_ref[...], NT)).T
+        d_ref[part, :] = dd
+        dp = (dd * tot_ref[part, :]).T
         dgeo = dgeo + jnp.where(member_ref[w] > 0.0, jnp.sum(dp, axis=0, keepdims=True), 0.0)
         dp = dp.astype(BF16)
-        dps.append(dp)
+        dp_ref[w] = dp
         feats_t = feats_ref[w].T
         for n, term in enumerate((dot(feats_t, dp, NN), dot(agg_t, du, NN))):
             grads_ref[n] = term if w == 0 else grads_ref[n] + term
     gslab_out[...] = dgeo
-    for w in range(walkers):
-        df_ref[w] = cot_ref[w].astype(F32) + dot(dps[w], ws_ref[...], NT)
+    dqt_ref[...] = jnp.zeros(dqt_ref.shape, F32)
 
     mine = pl.ds(pl.multiple_of(core * lanes, lanes), lanes)
     theirs = pl.ds(pl.multiple_of((1 - core) * lanes, lanes), lanes)
@@ -264,7 +262,7 @@
     for r in range(1, slabs):
         send(gslab_out, gslab_in.at[slab], 1, at(slab=lax.rem(slab + r, slabs)))
 
-    backward_pass(0, tiles // 2, d_ref, t_ref, v_ref)
+    backward_pass(0, groups // 2, d_ref, t_ref, slide_ref, v_ref, dqt_ref)
 
     cross.wait()
     half_us[...] = grads_ref[pl.ds(0, 2), :, mine] + core_in_us[...]
@@ -276,7 +274,7 @@
         to = lax.rem(chip + r, chips)
         send(plane_out.at[to], plane_in.at[chip], 2, chip_at(to, core))
 
-    backward_pass(tiles // 2, tiles // 2, d_ref, t_ref, v_ref)
+    backward_pass(groups // 2, groups // 2, d_ref, t_ref, slide_ref, v_ref, dqt_ref)
 
     settle(gslab_in.at[pl.ds(0, slabs - 1)], 1)
     gsum = gslab_in[0]
@@ -288,7 +286,7 @@
         send(gring_out, gring_in.at[z], 7, at(walker=lax.rem(z + r, walks)))
 
     for w in range(walkers):
-        dq = dot(v_ref[w * width : (w + 1) * width, :], slide_ref[...], NT).T
+        dq = dqt_ref[w * width : (w + 1) * width, :].T
         own_ref[w] = dq[RIM : RIM + rows]
         dqb = dq.astype(BF16)
         rim_out[0, w] = dqb[:RIM]
@@ -307,6 +305,10 @@
         to = lax.rem(z + r, walks)
         send(ring_out_p.at[to], ring_in_p.at[z], 6, at(walker=to))
 
+    for w in range(walkers):
+        newf_ref[w] = (feats_ref[w].astype(F32) + upd_ref[w]).astype(BF16)
+        df_ref[w] = cot_ref[w].astype(F32) + dot(dp_ref[w], ws_ref[...], NT)
+
     settle(plane_in.at[pl.ds(0, chips - 1)], 2)
     part = plane_in[0].astype(F32)
     for c in range(1, chips):
@@ -412,21 +414,20 @@
     scr = pltpu.VMEM
     dma = pltpu.SemaphoreType.DMA
     rim = sds((walkers, RIM, width), BF16)
-    before, after, weights, p, turn, slide, feats_v, inv, member = pl.pallas_call(
+    before, after, weights, p, slide, feats_v, inv, member = pl.pallas_call(
         functools.partial(first_kernel, slabs),
         out_shape=(
             rim,
             rim,
             sds((walkers, slots, rows), F32),
-            sds((walkers * width, STEPS * rows), F32),
-            sds((rows, STEPS * rows), BF16),
-            sds((wide, len(BASES) * wide), BF16),
+            sds((walkers * width, rows), F32),
+            sds((wide, SLOTS * rows), BF16),
             sds((walkers, rows, width), BF16),
             sds((walkers, rows), F32),
             sds((walkers, lats, width), F32),
         ),
         in_specs=hbm(7),
-        out_specs=vmem(9),
+        out_specs=vmem(8),
         scratch_shapes=[
             pltpu.SMEM((1, walkers), jnp.int32),
             scr((walkers, slots, rows), jnp.int32),
@@ -455,7 +456,7 @@
             sds((3, share_rows, width), F32),
             sds((lats, width), F32),
         ),
-        in_specs=vmem(9) + hbm(4),
+        in_specs=vmem(8) + hbm(4),
         out_specs=vmem(4),
         scratch_shapes=[
             scr((width, width), BF16),
@@ -464,12 +465,16 @@
             scr((walkers, rows, width), BF16),
             scr((walkers, wide, width), BF16),
             scr((walkers, width, wide), BF16),
-            scr((walkers * width, len(BASES) * wide), F32),
+            scr((walkers * width, wide), BF16),
+            scr((2, walkers * width, FGROUP * rows), F32),
             scr((slots, walkers * width, rows), F32),
-            scr((walkers * width, STEPS * rows), BF16),
-            scr((walkers * width, STEPS * rows), BF16),
-            scr((walkers * width, STEPS * rows), F32),
-            scr((walkers * width, len(BASES) * wide), BF16),
+            scr((walkers * width, rows), F32),
+            scr((walkers * width, rows), F32),
+            scr((walkers * width, rows), F32),
+            scr((2, walkers * width, BGROUP * rows), BF16),
+            scr((walkers * width, wide), F32),
+            scr((walkers, rows, width), F32),
+            scr((walkers, rows, width), BF16),
             scr((walkers, rows, width), F32),
             scr((2, walkers, RIM, width), BF16),
             scr((2, walkers, RIM, width), BF16),
@@ -498,7 +503,7 @@
         ],
         compiler_params=pltpu.CompilerParams(collective_id=1, has_side_effects=True, vmem_limit_bytes=44 * MIB),
         name="main",
-    )(before, after, weights, p, turn, slide, feats_v, inv, member, *far(w_self, w_pair, w_update, cot))
+    )(before, after, weights, p, slide, feats_v, inv, member, *far(w_self, w_pair, w_update, cot))
 
     block = sds((share_rows, width), F32)
     newf, df, gs, gp, gu, geo = pl.pallas_call(

time: 56.5 us -> 52.7 us (0.933)
  Pallas kernels: 55.7 us -> 51.9 us
    pallas_call x1, Pallas kernels: 45.8 us -> 42 us  [body(): pl.pallas_call(functools.partial(main_kernel, slabs, walks, geoms), out_s...]
where the time goes in v4:
time: 52.7 us; the launch traced here: 52.5 us
  Pallas kernels  51.9 us (98%)
  between operations  0.65 us (1%)
    pallas_call x1, Pallas kernels, body(): pl.pallas_call(functools.partial(main_kernel, slabs, walks, geoms), out_s...  42 us
    pallas_call x1, Pallas kernels, body(): pl.pallas_call(functools.partial(first_kernel, slabs), out_shape=(rim, ri...  9.11 us

profile of v4, /device:TPU:1, one launch (start us, length us, event | category | flops | bytes accessed | tf_op | source)
XLA Modules:
  0.0 52.5 jit_solution(4174956184373756701)
XLA Ops:
  0.6 9.1 %first.1 = (bf16[2,32,256]{2,1,0:T(8,128)(2,1)S(1)}, bf16[2,32,256]{2,1,0:T(8,128)(2,1)S(1)}, f32[2,64,128]{2,1,0:T(8,128)S(1)}, f32[512,128]{1,0:T(8,128)S(1)},...) custom-call(s32[1,2]{1,0:T(1,128)} %lat_hbm.1, ...), custom_call_target="tpu_custom_call" | custom-call | tf_op jit(solution)/shard_map/first/pallas_call | solution.py:417
  9.8 42.0 %main.1 = (bf16[2,128,256]{2,1,0:T(8,128)(2,1)S(1)}, f32[2,128,256]{2,1,0:T(8,128)S(1)}, f32[3,16,256]{2,1,0:T(8,128)S(1)}, f32[2,256]{1,0:T(2,128)S(1)}) custom-call(bf16[2,32,256]{2,1,0:T(8,128)(2,1)S(1)} %get-tuple-element.24.before_ref, bf16[2,32,256]{2,1,0:T(8,128)(2,1)S(1)} %get-tuple-element.25.after_ref, f32[2,64,128]{2,1,0:T(8,128)S(1)} %get-tuple-element.26.w_ref, ...), custom_call_target="tpu_custom_call" | custom-call | tf_op jit(solution)/shard_map/main/pallas_call | solution.py:451
  51.7 0.8 %last.1 = (bf16[2,128,256]{2,1,0:T(8,128)(2,1)}, f32[2,128,256]{2,1,0:T(8,128)}, f32[16,256]{1,0:T(8,128)}, f32[16,256]{1,0:T(8,128)}, f32[16,256]{1,0:T(8,128)}, /*index=5*/f32[2,256]{1,0:T(2,128)}) custom-call(bf16[2,128,256]{2,1,0:T(8,128)(2,1)S(1)} %get-tuple-element.32.newf, f32[2,128,256]{2,1,0:T(8,128)S(1)} %get-tuple-element.33.df, ...), custom_call_target="tpu_custom_call" | custom-call | tf_op jit(solution)/shard_map/last/pallas_call | solution.py:509

commit v5 on v4

--- a/solution.py
+++ b/solution.py
@@ -100,19 +100,23 @@
     lax.fori_loop(0, groups // 2, step, 0)
 
 
-def backward_pass(first, count, d_ref, t_ref, slide_ref, v_ref, dqt_ref):
-    total, rows = d_ref.shape
+def backward_pass(part, first, count, d_ref, t_ref, slide_ref, v_ref, dqt_ref):
+    rows = d_ref.shape[1]
+    lanes = dqt_ref.shape[1] // 2
+    width = 2 * lanes
 
     def work(g, at_slot):
-        for r in range(0, total, TILE):
-            here = slice(r, r + TILE)
-            d = d_ref[here, :]
-            for x in range(BGROUP):
-                v_ref[at_slot, here, x * rows : (x + 1) * rows] = (t_ref[g * BGROUP + x, here, :] * d).astype(BF16)
+        for w in range(2):
+            for r in range(0, lanes, TILE):
+                here = slice(w * width + part * lanes + r, w * width + part * lanes + r + TILE)
+                there = slice(w * lanes + r, w * lanes + r + TILE)
+                d = d_ref[here, :]
+                for x in range(BGROUP):
+                    v_ref[at_slot, there, x * rows : (x + 1) * rows] = (t_ref[g * BGROUP + x, here, :] * d).astype(BF16)
 
     def gather(g, at_slot):
         cols = pl.ds(pl.multiple_of(g * BGROUP * rows, BGROUP * rows), BGROUP * rows)
-        dqt_ref[...] += dot(v_ref[at_slot], slide_ref[:, cols], NT)
+        dqt_ref[part] += dot(v_ref[at_slot], slide_ref[:, cols], NT)
 
     work(first, 0)
 
@@ -175,7 +179,7 @@
     before_ref, after_ref, w_ref, p_ref, slide_ref, feats_ref, inv_ref, member_ref, ws_hbm, wp_hbm, wu_hbm, cot_hbm,
     newf_ref, df_ref, share_ref, geo_out_ref,
     ws_ref, wp_ref, wu_ref, cot_ref, ext_ref, ext_t_ref, q_ref, h_ref, t_ref, agg_ref, tot_ref, d_ref, v_ref, dqt_ref, upd_ref, dp_ref, own_ref,
-    rim_out, rim_in, grads_ref, half_us, half_p,
+    rim_out, rim_in, grads_ref, half_us, pair_ref,
     core_in_us, core_in_p, plane_out, plane_in, ring_out_us, ring_in_us, ring_out_p, ring_in_p,
     row_us, gather_us, row_p, gather_p, gslab_out, gslab_in, gring_out, gring_in,
     load_sem, send_sem, recv_sem,
@@ -208,10 +212,15 @@
         c.start()
         return c
 
+    def settle_send(ref, n):
+        pltpu.make_async_remote_copy(ref, ref, send_sem.at[n], recv_sem.at[n], **at(slab=nxt)).wait_send()
+
+    def settle_recv(ref, n):
+        pltpu.make_async_remote_copy(ref, ref, send_sem.at[n], recv_sem.at[n], **at(slab=nxt)).wait_recv()
+
     def settle(ref, n):
-        c = pltpu.make_async_remote_copy(ref, ref, send_sem.at[n], recv_sem.at[n], **at(slab=nxt))
-        c.wait_send()
-        c.wait_recv()
+        settle_send(ref, n)
+        settle_recv(ref, n)
 
     loads = []
     for n, (src, dst) in enumerate(((wp_hbm, wp_ref), (wu_hbm, wu_ref), (cot_hbm, cot_ref), (ws_hbm, ws_ref))):
@@ -262,7 +271,41 @@
     for r in range(1, slabs):
         send(gslab_out, gslab_in.at[slab], 1, at(slab=lax.rem(slab + r, slabs)))
 
-    backward_pass(0, groups // 2, d_ref, t_ref, slide_ref, v_ref, dqt_ref)
+    def pair_half(part):
+        term = None
+        for w in range(walkers):
+            dq = dqt_ref[part, w * lanes : (w + 1) * lanes, :].T
+            cols = slice(part * lanes, (part + 1) * lanes)
+            own_ref[w, :, cols] = dq[RIM : RIM + rows]
+            dqb = dq.astype(BF16)
+            rim_out[0, w, :, cols] = dqb[:RIM]
+            rim_out[1, w, :, cols] = dqb[RIM + rows : 2 * RIM + rows]
+            more = dot(ext_t_ref[w], dqb, NN)
+            term = more if w == 0 else term + more
+        pair_ref[part] = term.reshape(pair_ref.shape[1:])
+        return send(pair_ref.at[part, :, 1 - core], core_in_p.at[part], 3 + part, at(geom=pair + 1 - core))
+
+    owner = lax.rem(z + core, 2) == 0
+    zz = z // 2
+
+    def ring_half(part, cross):
+        cross.wait()
+        ring_out_p[part] = (pair_ref[part, :, core] + core_in_p[part]).astype(BF16)
+
+        @pl.when(owner)
+        def _():
+            ring_in_p[part, z] = ring_out_p[part, zz]
+
+        @pl.when(jnp.logical_not(owner))
+        def _():
+            send(ring_out_p.at[part, zz], ring_in_p.at[part, z], 11 + part, at(walker=2 * zz + core))
+
+        for r in range(1, walks // 2):
+            to = lax.rem(zz + r, walks // 2)
+            send(ring_out_p.at[part, to], ring_in_p.at[part, z], 11 + part, at(walker=2 * to + core))
+
+    backward_pass(0, 0, groups, d_ref, t_ref, slide_ref, v_ref, dqt_ref)
+    cross_p = pair_half(0)
 
     cross.wait()
     half_us[...] = grads_ref[pl.ds(0, 2), :, mine] + core_in_us[...]
@@ -274,8 +317,8 @@
         to = lax.rem(chip + r, chips)
         send(plane_out.at[to], plane_in.at[chip], 2, chip_at(to, core))
 
-    backward_pass(groups // 2, groups // 2, d_ref, t_ref, slide_ref, v_ref, dqt_ref)
-
+    backward_pass(1, 0, 2, d_ref, t_ref, slide_ref, v_ref, dqt_ref)
+    ring_half(0, cross_p)
     settle(gslab_in.at[pl.ds(0, slabs - 1)], 1)
     gsum = gslab_in[0]
     for s in range(1, slabs):
@@ -285,25 +328,11 @@
     for r in range(1, walks):
         send(gring_out, gring_in.at[z], 7, at(walker=lax.rem(z + r, walks)))
 
-    for w in range(walkers):
-        dq = dqt_ref[w * width : (w + 1) * width, :].T
-        own_ref[w] = dq[RIM : RIM + rows]
-        dqb = dq.astype(BF16)
-        rim_out[0, w] = dqb[:RIM]
-        rim_out[1, w] = dqb[RIM + rows : 2 * RIM + rows]
-        term = dot(ext_t_ref[w], dqb, NN)
-        grads_ref[2] = term if w == 0 else grads_ref[2] + term
-    cross = send(grads_ref.at[2, :, theirs], core_in_p, 3, at(geom=pair + 1 - core))
-    down = send(rim_out.at[0], rim_in.at[0], 4, at(slab=prv))
-    up = send(rim_out.at[1], rim_in.at[1], 5, at(slab=nxt))
-    cross.wait()
-    half_p[...] = (grads_ref[2, :, mine] + core_in_p[...]).astype(BF16)
-    for v in range(walks):
-        ring_out_p[v] = half_p[pl.ds(v * (width // walks), width // walks), :]
-    ring_in_p[z] = ring_out_p[z]
-    for r in range(1, walks):
-        to = lax.rem(z + r, walks)
-        send(ring_out_p.at[to], ring_in_p.at[z], 6, at(walker=to))
+    backward_pass(1, 2, groups - 2, d_ref, t_ref, slide_ref, v_ref, dqt_ref)
+    cross_p = pair_half(1)
+    down = send(rim_out.at[0], rim_in.at[0], 5, at(slab=prv))
+    up = send(rim_out.at[1], rim_in.at[1], 6, at(slab=nxt))
+    ring_half(1, cross_p)
 
     for w in range(walkers):
         newf_ref[w] = (feats_ref[w].astype(F32) + upd_ref[w]).astype(BF16)
@@ -335,16 +364,26 @@
         df_ref[w] = df_ref[w] + dot(dq, wp_ref[...], NT)
 
     slot = core * chips + chip
-    settle(ring_in_p.at[pl.ds(0, walks - 1)], 6)
-    part = ring_in_p[0].astype(F32)
-    for v in range(1, walks):
-        part = part + ring_in_p[v].astype(F32)
-    row_p[...] = part.astype(BF16)
-    gather_p[slot] = row_p[...]
-    for k in range(2):
-        kk = core if k == 0 else 1 - core
-        for r in range(k ^ 1, chips):
-            send(row_p, gather_p.at[slot], 9, chip_at(lax.rem(chip + r, chips), kk))
+
+    for part in range(2):
+
+        @pl.when(jnp.logical_not(owner))
+        def _():
+            settle_send(ring_out_p.at[part], 11 + part)
+
+        @pl.when(owner)
+        def _():
+            settle_send(ring_out_p.at[part, pl.ds(0, walks // 2 - 1)], 11 + part)
+            settle_recv(ring_in_p.at[part, pl.ds(0, walks - 1)], 11 + part)
+            total = ring_in_p[part, 0].astype(F32)
+            for v in range(1, walks):
+                total = total + ring_in_p[part, v].astype(F32)
+            row_p[part] = total.astype(BF16)
+            gather_p[part * chips + chip] = row_p[part]
+            for k in range(2):
+                kk = core if k == 0 else 1 - core
+                for r in range(k ^ 1, chips):
+                    send(row_p.at[part], gather_p.at[part * chips + chip], 13 + part, chip_at(lax.rem(chip + r, chips), kk))
 
     settle(ring_in_us.at[pl.ds(0, walks - 1)], 8)
     row = ring_in_us[0]
@@ -363,12 +402,21 @@
         gsum = gsum + gring_in[v]
     geo_out_ref[...] = gsum
 
-    settle(gather_p.at[pl.ds(0, 2 * chips - 1)], 9)
-    for k in range(2):
-        part = gather_p[k * chips].astype(F32)
+    for part in range(2):
+
+        @pl.when(owner)
+        def _():
+            settle_recv(gather_p.at[pl.ds(0, chips - 1)], 13 + part)
+            settle_send(gather_p.at[pl.ds(0, 2 * chips - 1)], 13 + part)
+
+        @pl.when(jnp.logical_not(owner))
+        def _():
+            settle_recv(gather_p.at[pl.ds(0, chips)], 13 + part)
+
+        total = gather_p[part * chips].astype(F32)
         for c in range(1, chips):
-            part = part + gather_p[k * chips + c].astype(F32)
-        share_ref[1, :, pl.ds(k * lanes, lanes)] = part
+            total = total + gather_p[part * chips + c].astype(F32)
+        share_ref[1, :, part * lanes : (part + 1) * lanes] = total
     settle(gather_us.at[pl.ds(0, 2 * chips - 1)], 10)
     for n in range(2):
         for k in range(2):
@@ -471,35 +519,35 @@
             scr((walkers * width, rows), F32),
             scr((walkers * width, rows), F32),
             scr((walkers * width, rows), F32),
-            scr((2, walkers * width, BGROUP * rows), BF16),
-            scr((walkers * width, wide), F32),
+            scr((2, width, BGROUP * rows), BF16),
+            scr((2, width, wide), F32),
             scr((walkers, rows, width), F32),
             scr((walkers, rows, width), BF16),
             scr((walkers, rows, width), F32),
             scr((2, walkers, RIM, width), BF16),
             scr((2, walkers, RIM, width), BF16),
-            scr((3, width, width), F32),
+            scr((2, width, width), F32),
             scr((2, width, lanes), F32),
-            scr((width, lanes), BF16),
+            scr((2, walks // 2, 2, share_rows, lanes), F32),
             scr((2, width, lanes), F32),
-            scr((width, lanes), F32),
+            scr((2, walks // 2, share_rows, lanes), F32),
             scr((chips, 2, walks, lanes), BF16),
             scr((chips, 2, walks, lanes), BF16),
             scr((walks, 2, lanes), F32),
             scr((walks, 2, lanes), F32),
-            scr((walks, share_rows, lanes), BF16),
-            scr((walks, share_rows, lanes), BF16),
+            scr((2, walks // 2, share_rows, lanes), BF16),
+            scr((2, walks, share_rows, lanes), BF16),
             scr((2, lanes), F32),
             scr((2 * chips, 2, lanes), F32),
-            scr((share_rows, lanes), BF16),
+            scr((2, share_rows, lanes), BF16),
             scr((2 * chips, share_rows, lanes), BF16),
             scr((lats, width), F32),
             scr((slabs, lats, width), F32),
             scr((lats, width), F32),
             scr((walks, lats, width), F32),
             dma((4,)),
-            dma((11,)),
-            dma((11,)),
+            dma((15,)),
+            dma((15,)),
         ],
         compiler_params=pltpu.CompilerParams(collective_id=1, has_side_effects=True, vmem_limit_bytes=44 * MIB),
         name="main",

time: 52.7 us -> 52.7 us (level)
  no operation moved by 1% of the time
where the time goes in v5:
time: 52.7 us; the launch traced here: 52.5 us
  Pallas kernels  51.8 us (98%)
  between operations  0.65 us (1%)
    pallas_call x1, Pallas kernels, body(): pl.pallas_call(functools.partial(main_kernel, slabs, walks, geoms), out_s...  41.9 us
    pallas_call x1, Pallas kernels, body(): pl.pallas_call(functools.partial(first_kernel, slabs), out_shape=(rim, ri...  9.11 us

profile of v5, /device:TPU:1, one launch (start us, length us, event | category | flops | bytes accessed | tf_op | source)
XLA Modules:
  0.0 52.5 jit_solution(6883251715668319368)
XLA Ops:
  0.6 9.1 %first.1 = (bf16[2,32,256]{2,1,0:T(8,128)(2,1)S(1)}, bf16[2,32,256]{2,1,0:T(8,128)(2,1)S(1)}, f32[2,64,128]{2,1,0:T(8,128)S(1)}, f32[512,128]{1,0:T(8,128)S(1)},...) custom-call(s32[1,2]{1,0:T(1,128)} %lat_hbm.1, ...), custom_call_target="tpu_custom_call" | custom-call | tf_op jit(solution)/shard_map/first/pallas_call | solution.py:465
  9.8 41.9 %main.1 = (bf16[2,128,256]{2,1,0:T(8,128)(2,1)S(1)}, f32[2,128,256]{2,1,0:T(8,128)S(1)}, f32[3,16,256]{2,1,0:T(8,128)S(1)}, f32[2,256]{1,0:T(2,128)S(1)}) custom-call(bf16[2,32,256]{2,1,0:T(8,128)(2,1)S(1)} %get-tuple-element.24.before_ref, bf16[2,32,256]{2,1,0:T(8,128)(2,1)S(1)} %get-tuple-element.25.after_ref, f32[2,64,128]{2,1,0:T(8,128)S(1)} %get-tuple-element.26.w_ref, ...), custom_call_target="tpu_custom_call" | custom-call | tf_op jit(solution)/shard_map/main/pallas_call | solution.py:499
  51.7 0.8 %last.1 = (bf16[2,128,256]{2,1,0:T(8,128)(2,1)}, f32[2,128,256]{2,1,0:T(8,128)}, f32[16,256]{1,0:T(8,128)}, f32[16,256]{1,0:T(8,128)}, f32[16,256]{1,0:T(8,128)}, /*index=5*/f32[2,256]{1,0:T(2,128)}) custom-call(bf16[2,128,256]{2,1,0:T(8,128)(2,1)S(1)} %get-tuple-element.32.newf, f32[2,128,256]{2,1,0:T(8,128)S(1)} %get-tuple-element.33.df, ...), custom_call_target="tpu_custom_call" | custom-call | tf_op jit(solution)/shard_map/last/pallas_call | solution.py:557

commit v6 on v5

--- a/solution.py
+++ b/solution.py
@@ -132,8 +132,8 @@
 
 
 def first_kernel(
-    slabs, lat_hbm, feats_hbm, nbr_hbm, env_hbm, cnt_hbm, ws_hbm, geo_hbm,
-    before_ref, after_ref, w_ref, p_ref, slide_ref, feats_ref, inv_ref, member_ref,
+    slabs, lat_hbm, feats_hbm, nbr_hbm, env_hbm, cnt_hbm, ws_hbm, geo_hbm, wp_hbm,
+    ext_ref, w_ref, p_ref, slide_ref, feats_ref, feats_t_ref, inv_ref, member_ref, wp_ref,
     lat_ref, nbr_ref, env_ref, cnt_ref, ws_ref, geo_ref, off_ref, wt_ref, load_sem, send_sem, recv_sem,
 ):
     me = lax.axis_index("slab")
@@ -143,7 +143,7 @@
     pl.semaphore_signal(barrier, inc=1, **at(slab=prv))
     loads = []
     for n, (src, dst) in enumerate((
-        (feats_hbm, feats_ref), (nbr_hbm, nbr_ref), (env_hbm, env_ref), (cnt_hbm, cnt_ref), (ws_hbm, ws_ref), (geo_hbm, geo_ref), (lat_hbm, lat_ref),
+        (feats_hbm, feats_ref), (nbr_hbm, nbr_ref), (env_hbm, env_ref), (cnt_hbm, cnt_ref), (ws_hbm, ws_ref), (geo_hbm, geo_ref), (lat_hbm, lat_ref), (wp_hbm, wp_ref),
     )):
         loads.append(pltpu.make_async_copy(src, dst, load_sem.at[n]))
         loads[-1].start()
@@ -152,10 +152,10 @@
         c.wait()
     pl.semaphore_wait(barrier, 2)
     up = pltpu.make_async_remote_copy(
-        feats_ref.at[:, pl.ds(rows - RIM, RIM)], before_ref, send_sem.at[0], recv_sem.at[0], **at(slab=nxt)
+        feats_ref.at[:, pl.ds(rows - RIM, RIM)], ext_ref.at[:, pl.ds(0, RIM)], send_sem.at[0], recv_sem.at[0], **at(slab=nxt)
     )
     down = pltpu.make_async_remote_copy(
-        feats_ref.at[:, pl.ds(0, RIM)], after_ref, send_sem.at[1], recv_sem.at[1], **at(slab=prv)
+        feats_ref.at[:, pl.ds(0, RIM)], ext_ref.at[:, pl.ds(rows + RIM, RIM)], send_sem.at[1], recv_sem.at[1], **at(slab=prv)
     )
     up.start()
     down.start()
@@ -170,15 +170,19 @@
         row = jnp.sum(jnp.where(member > 0.0, geo, 0.0), axis=0, keepdims=True)
         p = 0.5 * (dot(feats_ref[w], ws_ref[...], NN) + row)
         p_ref[w * width : (w + 1) * width, :] = p.T
+        feats_t_ref[w] = feats_ref[w].T
+        ext_ref[w, pl.ds(RIM, rows), :] = feats_ref[w]
+        pad = ext_ref.shape[1] - rows - 2 * RIM
+        ext_ref[w, pl.ds(rows + 2 * RIM, pad), :] = jnp.zeros((pad, width), BF16)
     up.wait()
     down.wait()
 
 
 def main_kernel(
     slabs, walks, geoms,
-    before_ref, after_ref, w_ref, p_ref, slide_ref, feats_ref, inv_ref, member_ref, ws_hbm, wp_hbm, wu_hbm, cot_hbm,
+    ext_ref, w_ref, p_ref, slide_ref, feats_ref, feats_t_ref, inv_ref, member_ref, wp_ref, ws_hbm, wu_hbm, cot_hbm,
     newf_ref, df_ref, share_ref, geo_out_ref,
-    ws_ref, wp_ref, wu_ref, cot_ref, ext_ref, ext_t_ref, q_ref, h_ref, t_ref, agg_ref, tot_ref, d_ref, v_ref, dqt_ref, upd_ref, dp_ref, own_ref,
+    ws_ref, wu_ref, cot_ref, q_ref, h_ref, t_ref, agg_ref, tot_ref, d_ref, v_ref, dqt_ref, upd_ref, dp_ref, own_ref,
     rim_out, rim_in, grads_ref, half_us, pair_ref,
     core_in_us, core_in_p, plane_out, plane_in, ring_out_us, ring_in_us, ring_out_p, ring_in_p,
     row_us, gather_us, row_p, gather_p, gslab_out, gslab_in, gring_out, gring_in,
@@ -223,25 +227,18 @@
         settle_recv(ref, n)
 
     loads = []
-    for n, (src, dst) in enumerate(((wp_hbm, wp_ref), (wu_hbm, wu_ref), (cot_hbm, cot_ref), (ws_hbm, ws_ref))):
+    for n, (src, dst) in enumerate(((wu_hbm, wu_ref), (cot_hbm, cot_ref), (ws_hbm, ws_ref))):
         loads.append(pltpu.make_async_copy(src, dst, load_sem.at[n]))
         loads[-1].start()
 
-    wide = ext_ref.shape[1]
     for w in range(walkers):
-        ext_ref[w, pl.ds(0, RIM), :] = before_ref[w]
-        ext_ref[w, pl.ds(RIM, rows), :] = feats_ref[w]
-        ext_ref[w, pl.ds(RIM + rows, RIM), :] = after_ref[w]
-        ext_ref[w, pl.ds(2 * RIM + rows, wide - rows - 2 * RIM), :] = jnp.zeros((wide - rows - 2 * RIM, width), BF16)
+        q = (0.5 * dot(ext_ref[w], wp_ref[...], NN)).astype(BF16)
+        q_ref[w * width : (w + 1) * width, :] = q.T
+
+    forward_pass(q_ref, p_ref, w_ref, slide_ref, h_ref, t_ref, agg_ref, tot_ref)
+
     for c in loads:
         c.wait()
-    for w in range(walkers):
-        q = (0.5 * dot(ext_ref[w], wp_ref[...], NN)).astype(BF16)
-        ext_t_ref[w] = ext_ref[w].T
-        q_ref[w * width : (w + 1) * width, :] = q.T
-
-    forward_pass(q_ref, p_ref, w_ref, slide_ref, h_ref, t_ref, agg_ref, tot_ref)
-
     dgeo = jnp.zeros((lats, width), F32)
     for w in range(walkers):
         part = slice(w * width, (w + 1) * width)
@@ -257,8 +254,7 @@
         dgeo = dgeo + jnp.where(member_ref[w] > 0.0, jnp.sum(dp, axis=0, keepdims=True), 0.0)
         dp = dp.astype(BF16)
         dp_ref[w] = dp
-        feats_t = feats_ref[w].T
-        for n, term in enumerate((dot(feats_t, dp, NN), dot(agg_t, du, NN))):
+        for n, term in enumerate((dot(feats_t_ref[w], dp, NN), dot(agg_t, du, NN))):
             grads_ref[n] = term if w == 0 else grads_ref[n] + term
     gslab_out[...] = dgeo
     dqt_ref[...] = jnp.zeros(dqt_ref.shape, F32)
@@ -280,7 +276,7 @@
             dqb = dq.astype(BF16)
             rim_out[0, w, :, cols] = dqb[:RIM]
             rim_out[1, w, :, cols] = dqb[RIM + rows : 2 * RIM + rows]
-            more = dot(ext_t_ref[w], dqb, NN)
+            more = dot(ext_ref[w].T, dqb, NN)
             term = more if w == 0 else term + more
         pair_ref[part] = term.reshape(pair_ref.shape[1:])
         return send(pair_ref.at[part, :, 1 - core], core_in_p.at[part], 3 + part, at(geom=pair + 1 - core))
@@ -304,8 +300,7 @@
             to = lax.rem(zz + r, walks // 2)
             send(ring_out_p.at[part, to], ring_in_p.at[part, z], 11 + part, at(walker=2 * to + core))
 
-    backward_pass(0, 0, groups, d_ref, t_ref, slide_ref, v_ref, dqt_ref)
-    cross_p = pair_half(0)
+    backward_pass(0, 0, groups // 2, d_ref, t_ref, slide_ref, v_ref, dqt_ref)
 
     cross.wait()
     half_us[...] = grads_ref[pl.ds(0, 2), :, mine] + core_in_us[...]
@@ -317,6 +312,8 @@
         to = lax.rem(chip + r, chips)
         send(plane_out.at[to], plane_in.at[chip], 2, chip_at(to, core))
 
+    backward_pass(0, groups // 2, groups // 2, d_ref, t_ref, slide_ref, v_ref, dqt_ref)
+    cross_p = pair_half(0)
     backward_pass(1, 0, 2, d_ref, t_ref, slide_ref, v_ref, dqt_ref)
     ring_half(0, cross_p)
     settle(gslab_in.at[pl.ds(0, slabs - 1)], 1)
@@ -461,21 +458,21 @@
     sds = jax.ShapeDtypeStruct
     scr = pltpu.VMEM
     dma = pltpu.SemaphoreType.DMA
-    rim = sds((walkers, RIM, width), BF16)
-    before, after, weights, p, slide, feats_v, inv, member = pl.pallas_call(
+    ext, weights, p, slide, feats_v, feats_t, inv, member, wp_v = pl.pallas_call(
         functools.partial(first_kernel, slabs),
         out_shape=(
-            rim,
-            rim,
+            sds((walkers, wide, width), BF16),
             sds((walkers, slots, rows), F32),
             sds((walkers * width, rows), F32),
             sds((wide, SLOTS * rows), BF16),
             sds((walkers, rows, width), BF16),
+            sds((walkers, width, rows), BF16),
             sds((walkers, rows), F32),
             sds((walkers, lats, width), F32),
+            sds((width, width), BF16),
         ),
-        in_specs=hbm(7),
-        out_specs=vmem(8),
+        in_specs=hbm(8),
+        out_specs=vmem(9),
         scratch_shapes=[
             pltpu.SMEM((1, walkers), jnp.int32),
             scr((walkers, slots, rows), jnp.int32),
@@ -485,13 +482,13 @@
             scr((lats, width), F32),
             scr((slots, rows), jnp.int32),
             scr((slots, rows), F32),
-            dma((7,)),
+            dma((8,)),
             dma((2,)),
             dma((2,)),
         ],
         compiler_params=pltpu.CompilerParams(collective_id=0, has_side_effects=True, vmem_limit_bytes=12 * MIB),
         name="first",
-    )(*far(lattice, feats, nbr, env, counts[0], w_self, geo_embed[0]))
+    )(*far(lattice, feats, nbr, env, counts[0], w_self, geo_embed[0], w_pair))
 
     chips = slabs * geoms // 2
     lanes = width // 2
@@ -504,15 +501,12 @@
             sds((3, share_rows, width), F32),
             sds((lats, width), F32),
         ),
-        in_specs=vmem(8) + hbm(4),
+        in_specs=vmem(9) + hbm(3),
         out_specs=vmem(4),
         scratch_shapes=[
             scr((width, width), BF16),
             scr((width, width), BF16),
-            scr((width, width), BF16),
             scr((walkers, rows, width), BF16),
-            scr((walkers, wide, width), BF16),
-            scr((walkers, width, wide), BF16),
             scr((walkers * width, wide), BF16),
             scr((2, walkers * width, FGROUP * rows), F32),
             scr((slots, walkers * width, rows), F32),
@@ -545,13 +539,13 @@
             scr((slabs, lats, width), F32),
             scr((lats, width), F32),
             scr((walks, lats, width), F32),
-            dma((4,)),
+            dma((3,)),
             dma((15,)),
             dma((15,)),
         ],
         compiler_params=pltpu.CompilerParams(collective_id=1, has_side_effects=True, vmem_limit_bytes=44 * MIB),
         name="main",
-    )(before, after, weights, p, slide, feats_v, inv, member, *far(w_self, w_pair, w_update, cot))
+    )(ext, weights, p, slide, feats_v, feats_t, inv, member, wp_v, *far(w_self, w_update, cot))
 
     block = sds((share_rows, width), F32)
     newf, df, gs, gp, gu, geo = pl.pallas_call(

time: 52.7 us -> 52 us (0.987)
  Pallas kernels: 51.8 us -> 51.2 us
    pallas_call x1, Pallas kernels: 41.9 us -> 41.2 us  [body(): pl.pallas_call(functools.partial(main_kernel, slabs, walks, geoms), out_s...]
where the time goes in v6:
time: 52 us; the launch traced here: 51.8 us
  Pallas kernels  51.2 us (98%)
  between operations  0.65 us (1%)
    pallas_call x1, Pallas kernels, body(): pl.pallas_call(functools.partial(main_kernel, slabs, walks, geoms), out_s...  41.2 us
    pallas_call x1, Pallas kernels, body(): pl.pallas_call(functools.partial(first_kernel, slabs), out_shape=(sds((wa...  9.2 us

profile of v6, /device:TPU:1, one launch (start us, length us, event | category | flops | bytes accessed | tf_op | source)
XLA Modules:
  0.0 51.8 jit_solution(2794905636223260705)
XLA Ops:
  0.6 9.2 %first.1 = (bf16[2,256,256]{2,1,0:T(8,128)(2,1)S(1)}, f32[2,64,128]{2,1,0:T(8,128)S(1)}, f32[512,128]{1,0:T(8,128)S(1)}, bf16[256,8192]{1,0:T(8,128)(2,1)S(1)}, ...) custom-call(s32[1,2]{1,0:T(1,128)} %lat_hbm.1, ...), custom_call_target="tpu_custom_call" | custom-call | tf_op jit(solution)/shard_map/first/pallas_call | solution.py:461
  9.8 41.2 %main.1 = (bf16[2,128,256]{2,1,0:T(8,128)(2,1)S(1)}, f32[2,128,256]{2,1,0:T(8,128)S(1)}, f32[3,16,256]{2,1,0:T(8,128)S(1)}, f32[2,256]{1,0:T(2,128)S(1)}) custom-call(bf16[2,256,256]{2,1,0:T(8,128)(2,1)S(1)} %get-tuple-element.25.ext_ref, f32[2,64,128]{2,1,0:T(8,128)S(1)} %get-tuple-element.26.w_ref, f32[512,128]{1,0:T(8,128)S(1)} %get-tuple-element.27.p_ref, ...), custom_call_target="tpu_custom_call" | custom-call | tf_op jit(solution)/shard_map/main/pallas_call | solution.py:496
  51.0 0.8 %last.1 = (bf16[2,128,256]{2,1,0:T(8,128)(2,1)}, f32[2,128,256]{2,1,0:T(8,128)}, f32[16,256]{1,0:T(8,128)}, f32[16,256]{1,0:T(8,128)}, f32[16,256]{1,0:T(8,128)}, /*index=5*/f32[2,256]{1,0:T(2,128)}) custom-call(bf16[2,128,256]{2,1,0:T(8,128)(2,1)S(1)} %get-tuple-element.34.newf, f32[2,128,256]{2,1,0:T(8,128)S(1)} %get-tuple-element.35.df, ...), custom_call_target="tpu_custom_call" | custom-call | tf_op jit(solution)/shard_map/last/pallas_call | solution.py:551

commit v7 on v6

--- a/solution.py
+++ b/solution.py
@@ -184,7 +184,7 @@
     newf_ref, df_ref, share_ref, geo_out_ref,
     ws_ref, wu_ref, cot_ref, q_ref, h_ref, t_ref, agg_ref, tot_ref, d_ref, v_ref, dqt_ref, upd_ref, dp_ref, own_ref,
     rim_out, rim_in, grads_ref, half_us, pair_ref,
-    core_in_us, core_in_p, plane_out, plane_in, ring_out_us, ring_in_us, ring_out_p, ring_in_p,
+    core_out_us, core_in_us, core_in_p, plane_out, plane_in, ring_out_us, ring_in_us, ring_out_p, ring_in_p,
     row_us, gather_us, row_p, gather_p, gslab_out, gslab_in, gring_out, gring_in,
     load_sem, send_sem, recv_sem,
 ):
@@ -262,7 +262,8 @@
     mine = pl.ds(pl.multiple_of(core * lanes, lanes), lanes)
     theirs = pl.ds(pl.multiple_of((1 - core) * lanes, lanes), lanes)
     pl.semaphore_wait(barrier, 2 * chips - 1 + walks - 1)
-    cross = send(grads_ref.at[pl.ds(0, 2), :, theirs], core_in_us, 0, at(geom=pair + 1 - core))
+    core_out_us[...] = grads_ref[:, :, theirs].astype(BF16)
+    cross = send(core_out_us, core_in_us, 0, at(geom=pair + 1 - core))
     gslab_in[slab] = gslab_out[...]
     for r in range(1, slabs):
         send(gslab_out, gslab_in.at[slab], 1, at(slab=lax.rem(slab + r, slabs)))
@@ -303,7 +304,7 @@
     backward_pass(0, 0, groups // 2, d_ref, t_ref, slide_ref, v_ref, dqt_ref)
 
     cross.wait()
-    half_us[...] = grads_ref[pl.ds(0, 2), :, mine] + core_in_us[...]
+    half_us[...] = grads_ref[:, :, mine] + core_in_us[...].astype(F32)
     for c in range(chips):
         for n in range(2):
             plane_out[c, n] = half_us[n, pl.ds(c, walks, stride=chips), :].astype(BF16)
@@ -314,8 +315,9 @@
 
     backward_pass(0, groups // 2, groups // 2, d_ref, t_ref, slide_ref, v_ref, dqt_ref)
     cross_p = pair_half(0)
-    backward_pass(1, 0, 2, d_ref, t_ref, slide_ref, v_ref, dqt_ref)
+    backward_pass(1, 0, groups // 2, d_ref, t_ref, slide_ref, v_ref, dqt_ref)
     ring_half(0, cross_p)
+    backward_pass(1, groups // 2, groups // 2, d_ref, t_ref, slide_ref, v_ref, dqt_ref)
     settle(gslab_in.at[pl.ds(0, slabs - 1)], 1)
     gsum = gslab_in[0]
     for s in range(1, slabs):
@@ -324,8 +326,6 @@
     gring_in[z] = gsum
     for r in range(1, walks):
         send(gring_out, gring_in.at[z], 7, at(walker=lax.rem(z + r, walks)))
-
-    backward_pass(1, 2, groups - 2, d_ref, t_ref, slide_ref, v_ref, dqt_ref)
     cross_p = pair_half(1)
     down = send(rim_out.at[0], rim_in.at[0], 5, at(slab=prv))
     up = send(rim_out.at[1], rim_in.at[1], 6, at(slab=nxt))
@@ -523,7 +523,8 @@
             scr((2, width, width), F32),
             scr((2, width, lanes), F32),
             scr((2, walks // 2, 2, share_rows, lanes), F32),
-            scr((2, width, lanes), F32),
+            scr((2, width, lanes), BF16),
+            scr((2, width, lanes), BF16),
             scr((2, walks // 2, share_rows, lanes), F32),
             scr((chips, 2, walks, lanes), BF16),
             scr((chips, 2, walks, lanes), BF16),

time: 52 us -> 51.6 us (level)
  no operation moved by 1% of the time
where the time goes in v7:
time: 51.6 us; the launch traced here: 51.5 us
  Pallas kernels  50.8 us (98%)
  between operations  0.65 us (1%)
    pallas_call x1, Pallas kernels, body(): pl.pallas_call(functools.partial(main_kernel, slabs, walks, geoms), out_s...  40.8 us
    pallas_call x1, Pallas kernels, body(): pl.pallas_call(functools.partial(first_kernel, slabs), out_shape=(sds((wa...  9.2 us

profile of v7, /device:TPU:1, one launch (start us, length us, event | category | flops | bytes accessed | tf_op | source)
XLA Modules:
  0.0 51.5 jit_solution(7351401176920576892)
XLA Ops:
  0.6 9.2 %first.1 = (bf16[2,256,256]{2,1,0:T(8,128)(2,1)S(1)}, f32[2,64,128]{2,1,0:T(8,128)S(1)}, f32[512,128]{1,0:T(8,128)S(1)}, bf16[256,8192]{1,0:T(8,128)(2,1)S(1)}, ...) custom-call(s32[1,2]{1,0:T(1,128)} %lat_hbm.1, ...), custom_call_target="tpu_custom_call" | custom-call | tf_op jit(solution)/shard_map/first/pallas_call | solution.py:461
  9.8 40.8 %main.1 = (bf16[2,128,256]{2,1,0:T(8,128)(2,1)S(1)}, f32[2,128,256]{2,1,0:T(8,128)S(1)}, f32[3,16,256]{2,1,0:T(8,128)S(1)}, f32[2,256]{1,0:T(2,128)S(1)}) custom-call(bf16[2,256,256]{2,1,0:T(8,128)(2,1)S(1)} %get-tuple-element.25.ext_ref, f32[2,64,128]{2,1,0:T(8,128)S(1)} %get-tuple-element.26.w_ref, f32[512,128]{1,0:T(8,128)S(1)} %get-tuple-element.27.p_ref, ...), custom_call_target="tpu_custom_call" | custom-call | tf_op jit(solution)/shard_map/main/pallas_call | solution.py:496
  50.7 0.8 %last.1 = (bf16[2,128,256]{2,1,0:T(8,128)(2,1)}, f32[2,128,256]{2,1,0:T(8,128)}, f32[16,256]{1,0:T(8,128)}, f32[16,256]{1,0:T(8,128)}, f32[16,256]{1,0:T(8,128)}, /*index=5*/f32[2,256]{1,0:T(2,128)}) custom-call(bf16[2,128,256]{2,1,0:T(8,128)(2,1)S(1)} %get-tuple-element.34.newf, f32[2,128,256]{2,1,0:T(8,128)S(1)} %get-tuple-element.35.df, ...), custom_call_target="tpu_custom_call" | custom-call | tf_op jit(solution)/shard_map/last/pallas_call | solution.py:552

commit v8 on v7

--- a/solution.py
+++ b/solution.py
@@ -200,21 +200,36 @@
     lats = gslab_out.shape[0]
     groups = SLOTS // BGROUP
 
-    def chip_at(c, k):
-        return at(slab=c // half_geoms, geom=lax.rem(c, half_geoms) * 2 + k)
+    nx, ny = slabs // 2, 2 * half_geoms
+    px, py = lax.rem(slab, nx), slab // nx * half_geoms + pair // 2
+    offsets = [(dx, dy) for dx in range(nx) for dy in range(ny) if dx or dy]
+    offsets.sort(key=lambda o: -min(o[0], nx - o[0]) - min(o[1], ny - o[1]))
+    others = []
+    for dx, dy in offsets:
+        tx, ty = lax.rem(px + dx, nx), lax.rem(py + dy, ny)
+        others.append((ty // half_geoms * nx + tx, lax.rem(ty, half_geoms)))
+
+    def ring_order(n):
+        return sorted(range(1, n), key=lambda r: -min(r, n - r))
 
     barrier = pltpu.get_barrier_semaphore()
-    for k in range(2):
-        kk = core if k == 0 else 1 - core
-        for r in range(k ^ 1, chips):
-            pl.semaphore_signal(barrier, inc=1, **chip_at(lax.rem(chip + r, chips), kk))
-    for r in range(1, walks):
+    for to_slab, to_pair in others:
+        for k in range(2):
+            pl.semaphore_signal(barrier, inc=1, **at(slab=to_slab, geom=to_pair * 2 + k))
+    pl.semaphore_signal(barrier, inc=1, **at(geom=pair + 1 - core))
+    for r in ring_order(walks):
         pl.semaphore_signal(barrier, inc=1, **at(walker=lax.rem(z + r, walks)))
 
     def send(src, dst, n, where):
         c = pltpu.make_async_remote_copy(src, dst, send_sem.at[n], recv_sem.at[n], **where)
         c.start()
         return c
+
+    def spread(src, dst, n):
+        for to_slab, to_pair in others:
+            for k in range(2):
+                send(src, dst, n, at(slab=to_slab, geom=to_pair * 2 + k))
+        send(src, dst, n, at(geom=pair + 1 - core))
 
     def settle_send(ref, n):
         pltpu.make_async_remote_copy(ref, ref, send_sem.at[n], recv_sem.at[n], **at(slab=nxt)).wait_send()
@@ -293,13 +308,13 @@
         def _():
             ring_in_p[part, z] = ring_out_p[part, zz]
 
+        for r in ring_order(walks // 2):
+            to = lax.rem(zz + r, walks // 2)
+            send(ring_out_p.at[part, to], ring_in_p.at[part, z], 11 + part, at(walker=2 * to + core))
+
         @pl.when(jnp.logical_not(owner))
         def _():
             send(ring_out_p.at[part, zz], ring_in_p.at[part, z], 11 + part, at(walker=2 * zz + core))
-
-        for r in range(1, walks // 2):
-            to = lax.rem(zz + r, walks // 2)
-            send(ring_out_p.at[part, to], ring_in_p.at[part, z], 11 + part, at(walker=2 * to + core))
 
     backward_pass(0, 0, groups // 2, d_ref, t_ref, slide_ref, v_ref, dqt_ref)
 
@@ -309,9 +324,8 @@
         for n in range(2):
             plane_out[c, n] = half_us[n, pl.ds(c, walks, stride=chips), :].astype(BF16)
     plane_in[chip] = plane_out[chip]
-    for r in range(1, chips):
-        to = lax.rem(chip + r, chips)
-        send(plane_out.at[to], plane_in.at[chip], 2, chip_at(to, core))
+    for to_slab, to_pair in others:
+        send(plane_out.at[to_slab * half_geoms + to_pair], plane_in.at[chip], 2, at(slab=to_slab, geom=to_pair * 2 + core))
 
     backward_pass(0, groups // 2, groups // 2, d_ref, t_ref, slide_ref, v_ref, dqt_ref)
     cross_p = pair_half(0)
@@ -324,7 +338,7 @@
         gsum = gsum + gslab_in[s]
     gring_out[...] = gsum
     gring_in[z] = gsum
-    for r in range(1, walks):
+    for r in ring_order(walks):
         send(gring_out, gring_in.at[z], 7, at(walker=lax.rem(z + r, walks)))
     cross_p = pair_half(1)
     down = send(rim_out.at[0], rim_in.at[0], 5, at(slab=prv))
@@ -343,7 +357,7 @@
         for n in range(2):
             ring_out_us[v, pl.ds(n, 1), :] = part[n, v : v + 1, :]
     ring_in_us[z] = ring_out_us[z]
-    for r in range(1, walks):
+    for r in ring_order(walks):
         to = lax.rem(z + r, walks)
         send(ring_out_us.at[to], ring_in_us.at[z], 8, at(walker=to))
 
@@ -377,10 +391,7 @@
                 total = total + ring_in_p[part, v].astype(F32)
             row_p[part] = total.astype(BF16)
             gather_p[part * chips + chip] = row_p[part]
-            for k in range(2):
-                kk = core if k == 0 else 1 - core
-                for r in range(k ^ 1, chips):
-                    send(row_p.at[part], gather_p.at[part * chips + chip], 13 + part, chip_at(lax.rem(chip + r, chips), kk))
+            spread(row_p.at[part], gather_p.at[part * chips + chip], 13 + part)
 
     settle(ring_in_us.at[pl.ds(0, walks - 1)], 8)
     row = ring_in_us[0]
@@ -388,10 +399,7 @@
         row = row + ring_in_us[v]
     row_us[...] = row
     gather_us[slot] = row
-    for k in range(2):
-        kk = core if k == 0 else 1 - core
-        for r in range(k ^ 1, chips):
-            send(row_us, gather_us.at[slot], 10, chip_at(lax.rem(chip + r, chips), kk))
+    spread(row_us, gather_us.at[slot], 10)
 
     settle(gring_in.at[pl.ds(0, walks - 1)], 7)
     gsum = gring_in[0]

time: 51.6 us -> 50.9 us (0.986)
  Pallas kernels: 50.8 us -> 50.1 us
    pallas_call x1, Pallas kernels: 40.8 us -> 40.1 us  [body(): pl.pallas_call(functools.partial(main_kernel, slabs, walks, geoms), out_s...]
where the time goes in v8:
time: 50.9 us; the launch traced here: 50.8 us
  Pallas kernels  50.1 us (98%)
  between operations  0.65 us (1%)
    pallas_call x1, Pallas kernels, body(): pl.pallas_call(functools.partial(main_kernel, slabs, walks, geoms), out_s...  40.1 us
    pallas_call x1, Pallas kernels, body(): pl.pallas_call(functools.partial(first_kernel, slabs), out_shape=(sds((wa...  9.2 us

profile of v8, /device:TPU:1, one launch (start us, length us, event | category | flops | bytes accessed | tf_op | source)
XLA Modules:
  0.0 50.8 jit_solution(15001870916918069265)
XLA Ops:
  0.6 9.2 %first.1 = (bf16[2,256,256]{2,1,0:T(8,128)(2,1)S(1)}, f32[2,64,128]{2,1,0:T(8,128)S(1)}, f32[512,128]{1,0:T(8,128)S(1)}, bf16[256,8192]{1,0:T(8,128)(2,1)S(1)}, ...) custom-call(s32[1,2]{1,0:T(1,128)} %lat_hbm.1, ...), custom_call_target="tpu_custom_call" | custom-call | tf_op jit(solution)/shard_map/first/pallas_call | solution.py:469
  9.8 40.1 %main.1 = (bf16[2,128,256]{2,1,0:T(8,128)(2,1)S(1)}, f32[2,128,256]{2,1,0:T(8,128)S(1)}, f32[3,16,256]{2,1,0:T(8,128)S(1)}, f32[2,256]{1,0:T(2,128)S(1)}) custom-call(bf16[2,256,256]{2,1,0:T(8,128)(2,1)S(1)} %get-tuple-element.25.ext_ref, f32[2,64,128]{2,1,0:T(8,128)S(1)} %get-tuple-element.26.w_ref, f32[512,128]{1,0:T(8,128)S(1)} %get-tuple-element.27.p_ref, ...), custom_call_target="tpu_custom_call" | custom-call | tf_op jit(solution)/shard_map/main/pallas_call | solution.py:504
  50.0 0.8 %last.1 = (bf16[2,128,256]{2,1,0:T(8,128)(2,1)}, f32[2,128,256]{2,1,0:T(8,128)}, f32[16,256]{1,0:T(8,128)}, f32[16,256]{1,0:T(8,128)}, f32[16,256]{1,0:T(8,128)}, /*index=5*/f32[2,256]{1,0:T(2,128)}) custom-call(bf16[2,128,256]{2,1,0:T(8,128)(2,1)S(1)} %get-tuple-element.34.newf, f32[2,128,256]{2,1,0:T(8,128)S(1)} %get-tuple-element.35.df, ...), custom_call_target="tpu_custom_call" | custom-call | tf_op jit(solution)/shard_map/last/pallas_call | solution.py:560

commit v9 on v8

--- a/solution.py
+++ b/solution.py
@@ -148,6 +148,7 @@
         loads.append(pltpu.make_async_copy(src, dst, load_sem.at[n]))
         loads[-1].start()
     walkers, rows, width = feats_ref.shape
+    window_matrix(slide_ref)
     for c in loads:
         c.wait()
     pl.semaphore_wait(barrier, 2)
@@ -159,7 +160,6 @@
     )
     up.start()
     down.start()
-    window_matrix(slide_ref)
     geo = geo_ref[...]
     inv_ref[...] = 1.0 / cnt_ref[...].astype(F32)
     for w in range(walkers):

time: 50.9 us -> 50.9 us (level)
  no operation moved by 1% of the time
where the time goes in v9:
time: 50.9 us; the launch traced here: 50.8 us
  Pallas kernels  50.1 us (98%)
  between operations  0.65 us (1%)
    pallas_call x1, Pallas kernels, body(): pl.pallas_call(functools.partial(main_kernel, slabs, walks, geoms), out_s...  40 us
    pallas_call x1, Pallas kernels, body(): pl.pallas_call(functools.partial(first_kernel, slabs), out_shape=(sds((wa...  9.29 us

profile of v9, /device:TPU:1, one launch (start us, length us, event | category | flops | bytes accessed | tf_op | source)
XLA Modules:
  0.0 50.8 jit_solution(18014883972755241267)
XLA Ops:
  0.6 9.3 %first.1 = (bf16[2,256,256]{2,1,0:T(8,128)(2,1)S(1)}, f32[2,64,128]{2,1,0:T(8,128)S(1)}, f32[512,128]{1,0:T(8,128)S(1)}, bf16[256,8192]{1,0:T(8,128)(2,1)S(1)}, ...) custom-call(s32[1,2]{1,0:T(1,128)} %lat_hbm.1, ...), custom_call_target="tpu_custom_call" | custom-call | tf_op jit(solution)/shard_map/first/pallas_call | solution.py:469
  9.9 40.0 %main.1 = (bf16[2,128,256]{2,1,0:T(8,128)(2,1)S(1)}, f32[2,128,256]{2,1,0:T(8,128)S(1)}, f32[3,16,256]{2,1,0:T(8,128)S(1)}, f32[2,256]{1,0:T(2,128)S(1)}) custom-call(bf16[2,256,256]{2,1,0:T(8,128)(2,1)S(1)} %get-tuple-element.25.ext_ref, f32[2,64,128]{2,1,0:T(8,128)S(1)} %get-tuple-element.26.w_ref, f32[512,128]{1,0:T(8,128)S(1)} %get-tuple-element.27.p_ref, ...), custom_call_target="tpu_custom_call" | custom-call | tf_op jit(solution)/shard_map/main/pallas_call | solution.py:504
  50.0 0.8 %last.1 = (bf16[2,128,256]{2,1,0:T(8,128)(2,1)}, f32[2,128,256]{2,1,0:T(8,128)}, f32[16,256]{1,0:T(8,128)}, f32[16,256]{1,0:T(8,128)}, f32[16,256]{1,0:T(8,128)}, /*index=5*/f32[2,256]{1,0:T(2,128)}) custom-call(bf16[2,128,256]{2,1,0:T(8,128)(2,1)S(1)} %get-tuple-element.34.newf, f32[2,128,256]{2,1,0:T(8,128)S(1)} %get-tuple-element.35.df, ...), custom_call_target="tpu_custom_call" | custom-call | tf_op jit(solution)/shard_map/last/pallas_call | solution.py:560

commit v10 on v9

--- a/solution.py
+++ b/solution.py
@@ -332,14 +332,6 @@
     backward_pass(1, 0, groups // 2, d_ref, t_ref, slide_ref, v_ref, dqt_ref)
     ring_half(0, cross_p)
     backward_pass(1, groups // 2, groups // 2, d_ref, t_ref, slide_ref, v_ref, dqt_ref)
-    settle(gslab_in.at[pl.ds(0, slabs - 1)], 1)
-    gsum = gslab_in[0]
-    for s in range(1, slabs):
-        gsum = gsum + gslab_in[s]
-    gring_out[...] = gsum
-    gring_in[z] = gsum
-    for r in ring_order(walks):
-        send(gring_out, gring_in.at[z], 7, at(walker=lax.rem(z + r, walks)))
     cross_p = pair_half(1)
     down = send(rim_out.at[0], rim_in.at[0], 5, at(slab=prv))
     up = send(rim_out.at[1], rim_in.at[1], 6, at(slab=nxt))
@@ -360,6 +352,15 @@
     for r in ring_order(walks):
         to = lax.rem(z + r, walks)
         send(ring_out_us.at[to], ring_in_us.at[z], 8, at(walker=to))
+
+    settle(gslab_in.at[pl.ds(0, slabs - 1)], 1)
+    gsum = gslab_in[0]
+    for s in range(1, slabs):
+        gsum = gsum + gslab_in[s]
+    gring_out[...] = gsum
+    gring_in[z] = gsum
+    for r in ring_order(walks):
+        send(gring_out, gring_in.at[z], 7, at(walker=lax.rem(z + r, walks)))
 
     down.wait()
     up.wait()

time: 50.9 us -> 51.2 us (level)
  no operation moved by 1% of the time
where the time goes in v10:
time: 51.2 us; the launch traced here: 51 us
  Pallas kernels  50.4 us (98%)
  between operations  0.65 us (1%)
    pallas_call x1, Pallas kernels, body(): pl.pallas_call(functools.partial(main_kernel, slabs, walks, geoms), out_s...  40.3 us
    pallas_call x1, Pallas kernels, body(): pl.pallas_call(functools.partial(first_kernel, slabs), out_shape=(sds((wa...  9.29 us

profile of v10, /device:TPU:1, one launch (start us, length us, event | category | flops | bytes accessed | tf_op | source)
XLA Modules:
  0.0 51.0 jit_solution(13078740722985799761)
XLA Ops:
  0.6 9.3 %first.1 = (bf16[2,256,256]{2,1,0:T(8,128)(2,1)S(1)}, f32[2,64,128]{2,1,0:T(8,128)S(1)}, f32[512,128]{1,0:T(8,128)S(1)}, bf16[256,8192]{1,0:T(8,128)(2,1)S(1)}, ...) custom-call(s32[1,2]{1,0:T(1,128)} %lat_hbm.1, ...), custom_call_target="tpu_custom_call" | custom-call | tf_op jit(solution)/shard_map/first/pallas_call | solution.py:470
  9.9 40.3 %main.1 = (bf16[2,128,256]{2,1,0:T(8,128)(2,1)S(1)}, f32[2,128,256]{2,1,0:T(8,128)S(1)}, f32[3,16,256]{2,1,0:T(8,128)S(1)}, f32[2,256]{1,0:T(2,128)S(1)}) custom-call(bf16[2,256,256]{2,1,0:T(8,128)(2,1)S(1)} %get-tuple-element.25.ext_ref, f32[2,64,128]{2,1,0:T(8,128)S(1)} %get-tuple-element.26.w_ref, f32[512,128]{1,0:T(8,128)S(1)} %get-tuple-element.27.p_ref, ...), custom_call_target="tpu_custom_call" | custom-call | tf_op jit(solution)/shard_map/main/pallas_call | solution.py:505
  50.2 0.8 %last.1 = (bf16[2,128,256]{2,1,0:T(8,128)(2,1)}, f32[2,128,256]{2,1,0:T(8,128)}, f32[16,256]{1,0:T(8,128)}, f32[16,256]{1,0:T(8,128)}, f32[16,256]{1,0:T(8,128)}, /*index=5*/f32[2,256]{1,0:T(2,128)}) custom-call(bf16[2,128,256]{2,1,0:T(8,128)(2,1)S(1)} %get-tuple-element.34.newf, f32[2,128,256]{2,1,0:T(8,128)S(1)} %get-tuple-element.35.df, ...), custom_call_target="tpu_custom_call" | custom-call | tf_op jit(solution)/shard_map/last/pallas_call | solution.py:561
